TPU v7x, 256 devices: a whole 4x4x8 slice. The times are simulated.
256 devices in a mesh: lat: 16 (over y_hi, x, core), lon: 16 (over z, y_lo).
Axes of the slice: x: 4, y: 4 (y_hi: 2, y_lo: 2; y = y_hi * 2 + y_lo), z: 8, core: 2. Of those that a mesh axis runs over, the one named last changes fastest.
Arguments:
- levels_in: bfloat16 [13, 96, 192, 512], P(None, 'lat', 'lon'), may hold values from -6 to 6
- latent_queries: bfloat16 [2, 512], replicated, may hold values from -6 to 6
- enc_kv: bfloat16 [512, 1024], replicated, may hold values from -0.25 to 0.25
- enc_out: bfloat16 [512, 512], replicated, may hold values from -0.25 to 0.25
- enc_temp: float32 [16], replicated, may hold values from 0.5 to 10
- w_qkv: bfloat16 [512, 1536], replicated, may hold values from -0.25 to 0.25
- w_out: bfloat16 [512, 512], replicated, may hold values from -0.25 to 0.25
- swin_temp: float32 [16], replicated, may hold values from 0.5 to 10
- lat_shift: int32 [1], replicated, may hold values from 1 to 5
- lon_shift: int32 [1], replicated, may hold values from 1 to 11
- key_valid: int32 [96, 192], P('lat', 'lon'), may hold values 0 or 1
- output_grad: bfloat16 [2, 96, 192, 512], P(None, 'lat', 'lon'), may hold values from -6 to 6
Outputs:
- output: bfloat16 [2, 96, 192, 512], P(None, 'lat', 'lon')
- levels_grad: bfloat16 [13, 96, 192, 512], P(None, 'lat', 'lon')
- w_qkv_grad: float32 [786432], P(('lat', 'lon'))
- w_out_grad: float32 [262144], P(('lat', 'lon'))
All inputs are finite; a program needn't handle non-finite values. No bound on the sum of `key_valid` on one device may be relied on, other than what follows from the above.
Results may differ from a plain program's by a relative error of at most 0.03.
Values may be sent and summed in bfloat16 or wider, within the bound.
A program may use at most 128 MiB of HBM per device.

v0:
```python
import math

import jax
import jax.numpy as jnp
from jax import lax
from jax.sharding import PartitionSpec as P

WLAT = 6
WLON = 12


EPS = 1e-05
NEG = -1e30
GRAD_GAIN = 6.0


def passed_along(block, axis, distance):
    devices = range(lax.axis_size(axis))
    route = [((i - distance) % len(devices), i) for i in devices]
    return lax.ppermute(block, axis, route)


def narrow(values):
    return lax.optimization_barrier(values.astype(jnp.bfloat16)).astype(jnp.float32)


def layer_norm(values):
    row_mean = jnp.mean(values, -1, keepdims=True)
    centered = values - row_mean
    variance = jnp.mean(centered * centered, -1, keepdims=True)
    inverse = lax.rsqrt(variance + EPS)
    return (centered * inverse, inverse)


def norm_back(unit, inverse, gradient):
    mean_grad = jnp.mean(gradient, -1, keepdims=True)
    mean_cross = jnp.mean(gradient * unit, -1, keepdims=True)
    return inverse * (gradient - mean_grad - unit * mean_cross)


def attend(queries, key_part, value_part, allowed, logit_scale):
    scores = jnp.einsum("bqhe,bkhe->bhqk", queries, key_part, precision=lax.Precision.HIGHEST)
    scores = scores * logit_scale[None, :, None, None]
    if allowed is not None:
        scores = jnp.where(allowed[:, None], scores, NEG)
    row_peak = jnp.max(scores, -1, keepdims=True)
    exponent = jnp.exp(scores - row_peak)
    probability = exponent / jnp.sum(exponent, -1, keepdims=True)
    narrowed = narrow(probability)
    context = jnp.einsum("bhqk,bkhe->bqhe", narrowed, value_part, precision=lax.Precision.HIGHEST)
    return (context, probability, narrowed)


def attend_back(queries, key_part, value_part, probability, narrowed, context_grad, logit_scale):
    prob_grad = jnp.einsum(
        "bqhe,bkhe->bhqk", context_grad, value_part, precision=lax.Precision.HIGHEST
    )
    value_grad = jnp.einsum(
        "bhqk,bqhe->bkhe", narrowed, context_grad, precision=lax.Precision.HIGHEST
    )
    score_grad = probability * (prob_grad - jnp.sum(probability * prob_grad, -1, keepdims=True))
    score_grad = score_grad * logit_scale[None, :, None, None]
    query_grad = jnp.einsum(
        "bhqk,bkhe->bqhe", score_grad, key_part, precision=lax.Precision.HIGHEST
    )
    key_grad = jnp.einsum("bhqk,bqhe->bkhe", score_grad, queries, precision=lax.Precision.HIGHEST)
    return (query_grad, key_grad, value_grad)


def to_windows(field):
    level_count, row_count, col_count, last_dim = field.shape
    shaped = field.reshape(level_count, row_count // WLAT, WLAT, col_count // WLON, WLON, last_dim)
    shaped = shaped.transpose(1, 3, 0, 2, 4, 5)
    return shaped.reshape(
        row_count // WLAT * (col_count // WLON), level_count * WLAT * WLON, last_dim
    )


def from_windows(field, level_count, row_count, col_count):
    last_dim = field.shape[-1]
    shaped = field.reshape(row_count // WLAT, col_count // WLON, level_count, WLAT, WLON, last_dim)
    shaped = shaped.transpose(2, 0, 3, 1, 4, 5)
    return shaped.reshape(level_count, row_count, col_count, last_dim)


def encode(levels, latent_queries, enc_kv, enc_out, enc_temp):
    level_total, row_count, col_count, features = levels.shape
    latent_count = latent_queries.shape[0]
    head_count = enc_temp.shape[0]
    head_size = features // head_count
    patch_count = row_count * col_count
    key_value = jnp.dot(
        levels.reshape(level_total * patch_count, features),
        enc_kv,
        preferred_element_type=jnp.float32,
    ).astype(jnp.bfloat16)
    key_value = key_value.reshape(level_total, patch_count, 2, head_count, head_size).astype(
        jnp.float32
    )
    key_value = jnp.transpose(key_value, (1, 0, 2, 3, 4))
    queries = latent_queries.astype(jnp.float32).reshape(1, latent_count, head_count, head_size)
    queries = jnp.broadcast_to(queries, (patch_count, latent_count, head_count, head_size))
    logit_scale = enc_temp / math.sqrt(head_size)
    context, probability, narrowed = attend(
        queries, key_value[:, :, 0], key_value[:, :, 1], None, logit_scale
    )
    context16 = (
        jnp.transpose(context, (1, 0, 2, 3))
        .reshape(latent_count * patch_count, features)
        .astype(jnp.bfloat16)
    )
    mixed = jnp.dot(context16, enc_out, preferred_element_type=jnp.float32).reshape(
        latent_count, patch_count, features
    )
    encoded = (latent_queries.astype(jnp.float32)[:, None, :] + mixed).astype(jnp.bfloat16)
    encoded = encoded.reshape(latent_count, row_count, col_count, features)
    return (encoded, (queries, key_value, probability, narrowed, logit_scale))


def encode_back(saved, encoded_grad, enc_kv, enc_out):
    queries, key_value, probability, narrowed, logit_scale = saved
    patch_count, level_total = (key_value.shape[0], key_value.shape[1])
    latent_count, head_count, head_size = (queries.shape[1], queries.shape[2], queries.shape[3])
    features = head_count * head_size
    incoming = encoded_grad.reshape(latent_count * patch_count, features)
    context_grad = narrow(jnp.dot(incoming, enc_out.T, preferred_element_type=jnp.float32))
    context_grad = jnp.transpose(
        context_grad.reshape(latent_count, patch_count, head_count, head_size), (1, 0, 2, 3)
    )
    unused, key_grad, value_grad = attend_back(
        queries,
        key_value[:, :, 0],
        key_value[:, :, 1],
        probability,
        narrowed,
        context_grad,
        logit_scale,
    )
    kv_grad = jnp.stack([key_grad, value_grad], 2)
    kv_grad = (
        jnp.transpose(kv_grad, (1, 0, 2, 3, 4))
        .reshape(level_total * patch_count, 2 * features)
        .astype(jnp.bfloat16)
    )
    return jnp.dot(kv_grad, enc_kv.T, preferred_element_type=jnp.float32).astype(jnp.bfloat16)


def swin_forward(rolled, wrap_flag, key_mask, w_qkv, w_out, swin_temp):
    level_count, row_count, col_count, features = rolled.shape
    head_count = swin_temp.shape[0]
    head_size = features // head_count
    unit, inverse = layer_norm(rolled.astype(jnp.float32))
    normed = to_windows(unit.astype(jnp.bfloat16))
    win_count, tok_count = (normed.shape[0], normed.shape[1])
    flattened = normed.reshape(win_count * tok_count, features)
    projected = jnp.dot(flattened, w_qkv, preferred_element_type=jnp.float32).astype(jnp.bfloat16)
    projected = projected.reshape(win_count, tok_count, 3, head_count, head_size).astype(
        jnp.float32
    )
    flag_grid = jnp.broadcast_to(
        wrap_flag[None, :, None, None], (level_count, row_count, col_count, 1)
    )
    mask_grid = jnp.broadcast_to(key_mask[None, :, :, None], (level_count, row_count, col_count, 1))
    flag_win = to_windows(flag_grid)[:, :, 0]
    mask_win = to_windows(mask_grid)[:, :, 0]
    same_class = flag_win[:, :, None] == flag_win[:, None, :]
    diagonal = jnp.eye(tok_count, dtype=bool)[None]
    allowed = same_class & ((mask_win[:, None, :] == 1) | diagonal)
    logit_scale = swin_temp / math.sqrt(head_size)
    context, probability, narrowed = attend(
        projected[:, :, 0], projected[:, :, 1], projected[:, :, 2], allowed, logit_scale
    )
    context16 = context.reshape(win_count * tok_count, features).astype(jnp.bfloat16)
    attended = jnp.dot(context16, w_out, preferred_element_type=jnp.float32).astype(jnp.bfloat16)
    attended = from_windows(
        attended.reshape(win_count, tok_count, features), level_count, row_count, col_count
    )
    return (
        attended,
        (unit, inverse, flattened, projected, probability, narrowed, context16, logit_scale),
    )


def swin_backward(saved, rolled_grad, w_qkv, w_out):
    unit, inverse, flattened, projected, probability, narrowed, context16, logit_scale = saved
    level_count, row_count, col_count, features = unit.shape
    win_count, tok_count = (projected.shape[0], projected.shape[1])
    head_count, head_size = (projected.shape[3], projected.shape[4])
    incoming = to_windows(rolled_grad).reshape(win_count * tok_count, features)
    term_out = lax.dot_general(
        context16, incoming, (((0,), (0,)), ((), ())), preferred_element_type=jnp.float32
    )
    context_grad = narrow(jnp.dot(incoming, w_out.T, preferred_element_type=jnp.float32))
    context_grad = context_grad.reshape(win_count, tok_count, head_count, head_size)
    query_grad, key_grad, value_grad = attend_back(
        projected[:, :, 0],
        projected[:, :, 1],
        projected[:, :, 2],
        probability,
        narrowed,
        context_grad,
        logit_scale,
    )
    qkv_grad = (
        jnp.stack([query_grad, key_grad, value_grad], 2)
        .reshape(win_count * tok_count, 3 * features)
        .astype(jnp.bfloat16)
    )
    term_qkv = lax.dot_general(
        flattened, qkv_grad, (((0,), (0,)), ((), ())), preferred_element_type=jnp.float32
    )
    unit_grad = jnp.dot(qkv_grad, w_qkv.T, preferred_element_type=jnp.float32)
    unit_grad = from_windows(
        unit_grad.reshape(win_count, tok_count, features), level_count, row_count, col_count
    )
    rolled_x_grad = norm_back(unit, inverse, unit_grad).astype(jnp.bfloat16)
    return (rolled_x_grad, term_qkv, term_out)


def to_rolled(field, lat_offset, lon_offset):
    level_count, row_count, col_count, features = field.shape
    east_part = passed_along(field[:, :, : WLON - 1], "lon", -1)
    widened = jnp.concatenate([field, east_part], 2)
    north_part = passed_along(widened[:, : WLAT - 1], "lat", -1)
    assembled = jnp.concatenate([widened, north_part], 1)
    return lax.dynamic_slice(
        assembled, (0, lat_offset, lon_offset, 0), (level_count, row_count, col_count, features)
    )


def from_rolled(field, lat_offset, lon_offset):
    level_count, row_count, col_count, features = field.shape
    west_part = passed_along(field[:, :, col_count - (WLON - 1) :], "lon", 1)
    widened = jnp.concatenate([west_part, field], 2)
    south_part = passed_along(widened[:, row_count - (WLAT - 1) :], "lat", 1)
    assembled = jnp.concatenate([south_part, widened], 1)
    return lax.dynamic_slice(
        assembled,
        (0, WLAT - 1 - lat_offset, WLON - 1 - lon_offset, 0),
        (level_count, row_count, col_count, features),
    )


def local(
    levels_in,
    latent_queries,
    enc_kv,
    enc_out,
    enc_temp,
    w_qkv,
    w_out,
    swin_temp,
    lat_shift,
    lon_shift,
    key_valid,
    output_grad,
):
    encoded, enc_saved = encode(levels_in, latent_queries, enc_kv, enc_out, enc_temp)
    level_count, row_count, col_count, features = encoded.shape
    lat_offset = lat_shift[0]
    lon_offset = lon_shift[0]
    rolled = to_rolled(encoded, lat_offset, lon_offset)
    lat_total = lax.axis_size("lat") * row_count
    row_index = lax.axis_index("lat") * row_count + jnp.arange(row_count, dtype=jnp.int32)
    wrap_flag = (row_index >= lat_total - lat_offset).astype(jnp.int32)
    attended, swin_saved = swin_forward(rolled, wrap_flag, key_valid, w_qkv, w_out, swin_temp)
    returned = from_rolled(attended, lat_offset, lon_offset)
    output = (encoded.astype(jnp.float32) + returned.astype(jnp.float32)).astype(jnp.bfloat16)
    rolled_grad = to_rolled(output_grad, lat_offset, lon_offset)
    rolled_x_grad, term_qkv, term_out = swin_backward(swin_saved, rolled_grad, w_qkv, w_out)
    returned_grad = from_rolled(rolled_x_grad, lat_offset, lon_offset)
    encoded_grad = (output_grad.astype(jnp.float32) + returned_grad.astype(jnp.float32)).astype(
        jnp.bfloat16
    )
    levels_grad = encode_back(enc_saved, encoded_grad, enc_kv, enc_out).reshape(levels_in.shape)
    token_total = level_count * lat_total * col_count * lax.axis_size("lon")
    factor = GRAD_GAIN * token_total ** (-0.5)
    summed = (
        lax.psum_scatter(term_qkv.reshape(-1), ("lat", "lon"), scatter_dimension=0, tiled=True),
        lax.psum_scatter(term_out.reshape(-1), ("lat", "lon"), scatter_dimension=0, tiled=True),
    )
    return (output, levels_grad, summed[0] * factor, summed[1] * factor)


def solution(mesh):
    return jax.shard_map(
        local,
        mesh=mesh,
        in_specs=(
            P(None, "lat", "lon", None),
            P(),
            P(),
            P(),
            P(),
            P(),
            P(),
            P(),
            P(),
            P(),
            P("lat", "lon"),
            P(None, "lat", "lon", None),
        ),
        out_specs=(
            P(None, "lat", "lon", None),
            P(None, "lat", "lon", None),
            P(("lat", "lon")),
            P(("lat", "lon")),
        ),
        check_vma=False,
    )
```

profile of v0, /device:TPU:16, one launch (start us, length us, event | category | flops | bytes accessed | tf_op | source)
XLA Modules:
  0.0 400.3 jit_solution(7408800781851319419)
XLA Ops:
  7.2 1.8 slice.52
  9.0 6.6 %collective-permute-start.4 = (bf16[2,6,11,512]{3,0,2,1:T(2,128)(2,1)}, bf16[2,6,11,512]{3,0,2,1:T(2,128)(2,1)}, u32[]{:S(2)}, u32[]{:S(2)}) collective-permute-start(bf16[2,6,11,512]{3,0,2,1:T(2,128)(2,1)} %slice.52), channel_id=1, source_target_pairs={{1,0},{2,1},{3,2},{4,3},{5,4},{6,5},{7,6},{8,7},{9,8},{10,9},{11,1... | collective-permute-start | bytes 405512 | tf_op jit(solution)/shard_map/ppermute | solution.py:20
  15.6 0.8 broadcast_in_dim.16
  16.3 0.7 convert_element_type.128
  17.0 1.8 copy.57
  18.9 1.1 reshape.296
  20.0 2.7 convolution_convert_fusion.1
  22.7 7.8 %reshape.312 = bf16[13,72,2,16,32]{4,3,2,1,0:T(8,128)(2,1)} reshape(bf16[936,1024]{1,0:T(8,128)(2,1)S(1)} %convolution_convert_fusion.1) | data formatting | bytes 3833856 | tf_op jit(solution)/shard_map/reshape | solution.py:97
  30.5 16.0 %copy.96 = bf16[13,72,2,16,32]{4,0,3,1,2:T(8,128)(2,1)} copy(bf16[13,72,2,16,32]{4,3,2,1,0:T(8,128)(2,1)} %reshape.312) | data formatting | bytes 3833856 | tf_op jit(solution)/shard_map/reshape | solution.py:97
  46.5 0.6 copy-done.26
  47.1 9.8 %fusion.12 = f32[72,16,2,13]{3,2,1,0:T(2,128)S(1)} fusion(bf16[72,13,2,16,32]{4,1,3,0,2:T(8,128)(2,1)} %bitcast.142, f32[16]{0:T(128)S(1)} %broadcast_multiply_fusion.4, f32[2,16,32]{2,0,1:T(2,128)S(1)} %copy.60), kind=kOutput, calls=%fused_computation.27 | convolution fusion | flops 11531520 | bytes 4842560 | tf_op jit(solution)/shard_map/bqhe,bkhe->bhqk/dot_general | solution.py:42
  56.9 2.5 fusion.52
  59.4 2.5 fusion.51
  61.9 0.9 copy-done.4
  62.8 2.2 fusion.13
  65.0 1.6 copy.61
  67.0 0.8 collective-permute-start
  68.8 0.7 fusion.47
  70.4 1.0 constant_dynamic-update-slice_fusion.2
  71.6 1.5 collective-permute-start.5
  73.0 0.5 broadcast_multiply_fusion.3
  73.6 11.7 %collective-permute-start.1 = (bf16[2,5,23,512]{3,2,1,0:T(8,128)(2,1)S(1)}, bf16[2,5,23,512]{3,2,1,0:T(8,128)(2,1)}, u32[]{:S(2)}, u32[]{:S(2)}) collective-permute-start(bf16[2,5,23,512]{3,2,1,0:T(8,128)(2,1)S(1)} %pad_maximum_fusion.1), channel_id=1, source_target_pairs={{16,0},{32,16},{48,32},{64,48},{80,64},{96,80},{112,96},{128,112},... | collective-permute-start | bytes 706568 | tf_op jit(solution)/shard_map/ppermute | solution.py:20
  85.3 0.4 fusion.44
  85.7 0.3 convolution_convert_fusion.5
  86.2 2.8 collective-permute-done.1
  89.0 1.3 convert_reduce_fusion
  90.7 0.6 copy-done.16
  91.4 0.4 convolution_convert_fusion
  92.1 0.5 fusion.39
  92.6 0.5 fusion.38
  93.1 0.8 fusion.53
  93.9 0.6 multiply_reduce_fusion
  94.8 1.2 convolution_bitcast_fusion.1
  96.0 2.4 convolution_bitcast_fusion.2
  98.4 2.0 convolution_bitcast_fusion.3
  100.7 0.8 copy.97
  101.5 2.2 collective-permute-start.2
  103.7 2.2 maximum_convert_fusion
  105.9 2.1 copy.76
  108.0 2.4 convert_element_type.152
  110.5 1.9 fusion.49
  112.7 2.3 fusion.54
  115.3 4.4 %reshape.308 = f32[786432]{0:T(1024)} reshape(f32[512,1536]{1,0:T(8,128)} %fusion.54) | data formatting | bytes 6291456 | tf_op jit(solution)/shard_map/reshape | solution.py:279
  119.7 1.3 copy.92
  121.2 1.1 constant_dynamic-update-slice_fusion.1
  122.5 0.8 slice.63
  123.5 6.9 %collective-permute-done.7 = bf16[2,5,23,512]{3,2,1,0:T(8,128)(2,1)S(1)} collective-permute-done((bf16[2,5,23,512]{3,2,1,0:T(8,128)(2,1)S(1)}, bf16[2,5,23,512]{3,2,1,0:T(8,128)(2,1)S(1)}, u32[]{:S(2)}, u32[]{:S(2)}) %collective-permute-start.7) | collective-permute-done | bytes 235552 | tf_op jit(solution)/shard_map/ppermute | solution.py:20
  130.4 0.4 add_convert_fusion
  131.5 1.1 copy.78
  132.6 3.7 convert_bitcast_fusion
  136.3 6.3 %copy.81 = bf16[72,13,1,16,32]{0,4,3,2,1:T(8,128)(2,1)S(1)} copy(bf16[72,13,1,16,32]{4,1,3,0,2:T(8,128)(2,1)} %convert_bitcast_fusion) | data formatting | bytes 1916928 | tf_op jit(solution)/shard_map/stack | solution.py:139
  142.6 5.5 %multiply_reduce_fusion.1 = (f32[72,16,2]{2,1,0:T(8,128)S(1)}, f32[72,16,2,13]{3,2,1,0:T(2,128)S(1)}) fusion(f32[72,16,2,13]{3,2,1,0:T(2,128)} %get-tuple-element.23, bf16[72,2,16,32]{3,1,2,0:T(2,128)(2,1)S(1)} %copy.78, bf16[72,13,2,16,32]{4,1,3,0,2:T(8,128)(2,1)} %bitcast.143), kind=kOutput, calls=%fused_computation.38 | convolution fusion | flops 1974528 | bytes 6174720 | tf_op jit(solution)/shard_map/bqhe,bkhe->bhqk/dot_general | solution.py:55
  148.2 17.9 %convert_bitcast_fusion.1 = bf16[72,13,1,16,32]{4,1,3,0,2:T(8,128)(2,1)} fusion(f32[72,16,2,13]{3,2,1,0:T(2,128)S(1)} %copy-done.24, f32[72,16,2,13]{3,2,1,0:T(2,128)S(1)} %get-tuple-element.32, f32[16]{0:T(128)S(1)} %copy-done.34, f32[72,16,2]{2,1,0:T(8,128)S(1)} %get-tuple-element.31, f32[2,16,32]{2,0,1:T(2,128)S(1)} %copy-done.27), kind=kOutput, calls=%fused_computation.7 | convolution fusion | flops 12070656 | bytes 1211456 | tf_op jit(solution)/shard_map/bhqk,bqhe->bkhe/dot_general | solution.py:66
  166.0 7.1 %copy.80 = bf16[72,13,1,16,32]{0,4,3,2,1:T(8,128)(2,1)} copy(bf16[72,13,1,16,32]{4,1,3,0,2:T(8,128)(2,1)} %convert_bitcast_fusion.1) | data formatting | bytes 1916928 | tf_op jit(solution)/shard_map/stack | solution.py:139
  173.1 2.1 maximum_bitcast_fusion
  175.3 5.3 %copy.82 = bf16[13,72,2,16,32]{1,0,4,3,2:T(8,128)(2,1)} copy(bf16[13,72,2,16,32]{1,4,3,2,0:T(8,128)(2,1)S(1)} %maximum_bitcast_fusion) | data formatting | bytes 3833856 | tf_op jit(solution)/shard_map/convert_element_type | solution.py:143
  180.6 7.1 %convert_element_type.158 = bf16[936,1024]{0,1:T(8,128)(2,1)} reshape(bf16[13,72,2,16,32]{1,0,4,3,2:T(8,128)(2,1)} %copy.82) | data formatting | bytes 3833856 | tf_op jit(solution)/shard_map/convert_element_type | solution.py:143
  187.6 4.0 %convolution_convert_fusion.2 = bf16[936,512]{1,0:T(8,128)(2,1)} fusion(bf16[936,1024]{0,1:T(8,128)(2,1)} %convert_element_type.158, bf16[512,1024]{1,0:T(8,128)(2,1)S(1)} %copy-done.30), kind=kOutput, calls=%fused_computation.22 | convolution fusion | flops 981946368 | bytes 3923968 | tf_op jit(solution)/shard_map/dot_general | solution.py:145
  191.7 2.0 reshape.307
  193.6 1.6 copy.83
  195.2 1.0 add_convert_fusion.1
  196.2 194.2 %all-reduce.5.cloned.1.call-done = (f32[786432]{0:T(1024)}, f32[262144]{0:T(1024)}) async-done(((f32[786432]{0:T(1024)}, f32[262144]{0:T(1024)}), (f32[786432]{0:T(1024)}, f32[262144]{0:T(1024)})) %all-reduce.5.cloned.1.call-update) | async-done | bytes 4194320
  390.4 1.3 dynamic-slice_multiply_fusion
  391.7 1.3 dynamic-slice_multiply_fusion.1
  (115 shorter events, 4.4 us)
Async XLA Ops:
  7.2 84.2 %copy-start = (bf16[512,1536]{1,0:T(8,128)(2,1)S(1)}, bf16[512,1536]{1,0:T(8,128)(2,1)}, u32[]{:S(2)}) copy-start(bf16[512,1536]{1,0:T(8,128)(2,1)} %param.17) | copy-start | bytes 4718596
  7.2 383.3 %all-reduce.5.cloned.1.call-start = ((), (), s32[]{:S(2)}) async-start(), calls=%async_computation | async-start | bytes 8388608
  9.0 61.4 %collective-permute-start.4 = (bf16[2,6,11,512]{3,0,2,1:T(2,128)(2,1)}, bf16[2,6,11,512]{3,0,2,1:T(2,128)(2,1)}, u32[]{:S(2)}, u32[]{:S(2)}) collective-permute-start(bf16[2,6,11,512]{3,0,2,1:T(2,128)(2,1)} %slice.52), channel_id=1, source_target_pairs={{1,0},{2,1},{3,2},{4,3},{5,4},{6,5},{7,6},{8,7},{9,8},{10,9},{11,1... | collective-permute-start | bytes 405512 | tf_op jit(solution)/shard_map/ppermute | solution.py:20
  30.5 16.0 %copy-start.31 = (f32[16]{0:T(128)S(1)}, f32[16]{0:T(128)}, u32[]{:S(2)}) copy-start(f32[16]{0:T(128)} %param.16) | copy-start | bytes 196
  46.5 10.4 %copy-start.33 = (f32[16]{0:T(128)}, f32[16]{0:T(128)S(1)}, u32[]{:S(2)}) copy-start(f32[16]{0:T(128)S(1)} %broadcast_multiply_fusion.4) | copy-start | bytes 196
  46.5 0.6 copy-start.26
  47.1 15.7 %copy-start.2 = (bf16[13,72,2,16,32]{4,0,3,1,2:T(8,128)(2,1)S(1)}, bf16[13,72,2,16,32]{4,0,3,1,2:T(8,128)(2,1)}, u32[]{:S(2)}) copy-start(bf16[13,72,2,16,32]{4,0,3,1,2:T(8,128)(2,1)} %copy.96) | copy-start | bytes 5750788
  61.9 0.9 copy-start.4
  62.8 3.8 copy-start.10
  65.0 3.7 copy-start.28
  65.0 5.2 %copy-start.22 = (bf16[2,6,12,512]{3,0,2,1:T(2,128)(2,1)S(1)}, bf16[2,6,12,512]{3,0,2,1:T(2,128)(2,1)}, u32[]{:S(2)}) copy-start(bf16[2,6,12,512]{3,0,2,1:T(2,128)(2,1)} %param.23) | copy-start | bytes 442372
  65.0 8.0 %copy-start.32 = (f32[16]{0:T(128)S(1)}, f32[16]{0:T(128)}, u32[]{:S(2)}) copy-start(f32[16]{0:T(128)} %param.19) | copy-start | bytes 196
  66.6 19.1 %copy-start.8 = (bf16[512,512]{1,0:T(8,128)(2,1)S(1)}, bf16[512,512]{1,0:T(8,128)(2,1)}, u32[]{:S(2)}) copy-start(bf16[512,512]{1,0:T(8,128)(2,1)} %param.18) | copy-start | bytes 1572868
  67.0 3.2 copy-start.18
  67.0 6.5 %collective-permute-start = (bf16[2,6,11,512]{3,2,1,0:T(8,128)(2,1)S(1)}, bf16[2,6,11,512]{3,2,1,0:T(8,128)(2,1)S(1)}, u32[]{:S(2)}, u32[]{:S(2)}) collective-permute-start(bf16[2,6,11,512]{3,2,1,0:T(8,128)(2,1)S(1)} %bitcast.156), channel_id=1, source_target_pairs={{1,0},{2,1},{3,2},{4,3},{5,4},{6,5},{7,6},{8,7},{9,8},{10,9},{11,1... | collective-permute-start | bytes 405512 | tf_op jit(solution)/shard_map/ppermute | solution.py:20
  71.6 13.7 %collective-permute-start.5 = (bf16[2,5,23,512]{3,0,2,1:T(2,128)(2,1)S(1)}, bf16[2,5,23,512]{3,0,2,1:T(2,128)(2,1)S(1)}, u32[]{:S(2)}, u32[]{:S(2)}) collective-permute-start(bf16[2,5,23,512]{3,0,2,1:T(2,128)(2,1)S(1)} %slice.64), channel_id=1, source_target_pairs={{16,0},{32,16},{48,32},{64,48},{80,64},{96,80},{112,96},{128,112},... | collective-permute-start | bytes 706568 | tf_op jit(solution)/shard_map/ppermute | solution.py:20
  73.6 15.4 %collective-permute-start.1 = (bf16[2,5,23,512]{3,2,1,0:T(8,128)(2,1)S(1)}, bf16[2,5,23,512]{3,2,1,0:T(8,128)(2,1)}, u32[]{:S(2)}, u32[]{:S(2)}) collective-permute-start(bf16[2,5,23,512]{3,2,1,0:T(8,128)(2,1)S(1)} %pad_maximum_fusion.1), channel_id=1, source_target_pairs={{16,0},{32,16},{48,32},{64,48},{80,64},{96,80},{112,96},{128,112},... | collective-permute-start | bytes 706568 | tf_op jit(solution)/shard_map/ppermute | solution.py:20
  85.7 5.0 %copy-start.20 = (bf16[144,512]{1,0:T(8,128)(2,1)}, bf16[144,512]{1,0:T(8,128)(2,1)S(1)}, u32[]{:S(2)}) copy-start(bf16[144,512]{1,0:T(8,128)(2,1)S(1)} %reshape_reshape_transpose_reshape.7) | copy-start | bytes 442372
  90.7 0.6 copy-start.16
  92.0 1.1 copy-start.25
  92.0 1.1 copy-start.29
  94.8 5.6 %copy-start.6 = (bf16[16,32,144]{2,1,0:T(8,128)(2,1)}, bf16[16,32,144]{2,1,0:T(8,128)(2,1)S(1)}, u32[]{:S(2)}) copy-start(bf16[16,32,144]{2,1,0:T(8,128)(2,1)S(1)} %convolution_convert_fusion.3) | copy-start | bytes 442372
  98.4 2.0 copy-start.9
  100.7 3.1 copy-start.12
  101.5 19.6 %collective-permute-start.2 = (bf16[2,6,11,512]{3,0,2,1:T(2,128)(2,1)}, bf16[2,6,11,512]{3,0,2,1:T(2,128)(2,1)}, u32[]{:S(2)}, u32[]{:S(2)}) collective-permute-start(bf16[2,6,11,512]{3,0,2,1:T(2,128)(2,1)} %copy.97), channel_id=1, source_target_pairs={{15,0},{0,1},{1,2},{2,3},{3,4},{4,5},{5,6},{6,7},{7,8},{8,9},{9,10... | collective-permute-start | bytes 405512 | tf_op jit(solution)/shard_map/ppermute | solution.py:20
  110.5 2.3 copy-start.3
  110.5 2.3 copy-start.17
  112.6 2.5 copy-start.7
  112.6 2.5 copy-start.21
  112.6 8.4 %collective-permute-start.6 = (bf16[2,6,11,512]{3,2,1,0:T(8,128)(2,1)S(1)}, bf16[2,6,11,512]{3,2,1,0:T(8,128)(2,1)S(1)}, u32[]{:S(2)}, u32[]{:S(2)}) collective-permute-start(bf16[2,6,11,512]{3,2,1,0:T(8,128)(2,1)S(1)} %slice.65), channel_id=1, source_target_pairs={{15,0},{0,1},{1,2},{2,3},{3,4},{4,5},{5,6},{6,7},{7,8},{8,9},{9,10... | collective-permute-start | bytes 405512 | tf_op jit(solution)/shard_map/ppermute | solution.py:20
  121.0 1.3 copy-start.13
  121.0 9.4 %copy-start.23 = (bf16[2,6,12,512]{3,0,2,1:T(2,128)(2,1)S(1)}, bf16[2,6,12,512]{3,0,2,1:T(2,128)(2,1)}, u32[]{:S(2)}) copy-start(bf16[2,6,12,512]{3,0,2,1:T(2,128)(2,1)} %param.23) | copy-start | bytes 442372
  121.0 9.9 %copy-start.11 = (bf16[512,512]{1,0:T(8,128)(2,1)S(1)}, bf16[512,512]{1,0:T(8,128)(2,1)}, u32[]{:S(2)}) copy-start(bf16[512,512]{1,0:T(8,128)(2,1)} %param.15) | copy-start | bytes 1572868
  121.1 9.3 %collective-permute-start.7 = (bf16[2,5,23,512]{3,2,1,0:T(8,128)(2,1)S(1)}, bf16[2,5,23,512]{3,2,1,0:T(8,128)(2,1)S(1)}, u32[]{:S(2)}, u32[]{:S(2)}) collective-permute-start(bf16[2,5,23,512]{3,2,1,0:T(8,128)(2,1)S(1)} %pad_maximum_fusion), channel_id=1, source_target_pairs={{240,0},{0,16},{16,32},{32,48},{48,64},{64,80},{80,96},{96,112},{1... | collective-permute-start | bytes 706568 | tf_op jit(solution)/shard_map/ppermute | solution.py:20
  122.3 10.3 %copy-start.5 = (bf16[72,16,2,13]{3,2,1,0:T(2,128)(2,1)S(1)}, bf16[72,16,2,13]{3,2,1,0:T(2,128)(2,1)}, u32[]{:S(2)}) copy-start(bf16[72,16,2,13]{3,2,1,0:T(2,128)(2,1)} %copy-done.4) | copy-start | bytes 179716
  122.5 9.0 %copy-start.14 = (bf16[2,6,23,512]{3,0,2,1:T(2,128)(2,1)}, bf16[2,6,23,512]{3,0,2,1:T(2,128)(2,1)S(1)}, u32[]{:S(2)}) copy-start(bf16[2,6,23,512]{3,0,2,1:T(2,128)(2,1)S(1)} %constant_dynamic-update-slice_fusion) | copy-start | bytes 847876
  123.3 71.9 %collective-permute-start.3 = (bf16[2,5,23,512]{3,0,2,1:T(2,128)(2,1)}, bf16[2,5,23,512]{3,0,2,1:T(2,128)(2,1)S(1)}, u32[]{:S(2)}, u32[]{:S(2)}) collective-permute-start(bf16[2,5,23,512]{3,0,2,1:T(2,128)(2,1)} %slice.63), channel_id=1, source_target_pairs={{240,0},{0,16},{16,32},{32,48},{48,64},{64,80},{80,96},{96,112},{1... | collective-permute-start | bytes 706568 | tf_op jit(solution)/shard_map/ppermute | solution.py:20
  142.6 5.6 %copy-start.24 = (f32[72,16,2,13]{3,2,1,0:T(2,128)S(1)}, f32[72,16,2,13]{3,2,1,0:T(2,128)}, u32[]{:S(2)}) copy-start(f32[72,16,2,13]{3,2,1,0:T(2,128)} %get-tuple-element.23) | copy-start | bytes 359428
  142.6 5.6 %copy-start.27 = (f32[2,16,32]{2,0,1:T(2,128)S(1)}, f32[2,16,32]{2,0,1:T(2,128)}, u32[]{:S(2)}) copy-start(f32[2,16,32]{2,0,1:T(2,128)} %copy-done.26) | copy-start | bytes 12292
  142.6 5.6 %copy-start.34 = (f32[16]{0:T(128)S(1)}, f32[16]{0:T(128)}, u32[]{:S(2)}) copy-start(f32[16]{0:T(128)} %copy-done.33) | copy-start | bytes 196
  180.6 7.1 %copy-start.30 = (bf16[512,1024]{1,0:T(8,128)(2,1)S(1)}, bf16[512,1024]{1,0:T(8,128)(2,1)}, u32[]{:S(2)}) copy-start(bf16[512,1024]{1,0:T(8,128)(2,1)} %param.14) | copy-start | bytes 3145732
  187.6 205.4 %copy-start.1 = (bf16[512,1536]{1,0:T(8,128)(2,1)S(1)}, bf16[512,1536]{1,0:T(8,128)(2,1)}, u32[]{:S(2)}) copy-start(bf16[512,1536]{1,0:T(8,128)(2,1)} %param.17) | copy-start | bytes 4718596
  191.6 3.6 copy-start.15
  191.6 3.6 copy-start.19
Sparse Core Ops, SparseCore 0:
  121.1 269.2 all-reduce.4
where the time goes:
time: 404 us; the launch traced here: 400 us
  waiting for transfers between devices  204 us (50%)
  local copies, waits for them, and re-layouts  79.2 us (20%)
  matrix products  58.7 us (15%)
  starting transfers between devices  23.1 us (6%)
  other arithmetic  18.9 us (5%)
  between operations  16.5 us (4%)
    unnamed x2, waiting for transfers between devices  194 us
    reshape x2, local copies, waits for them, and re-layouts, encode(): key_value.reshape(level_total, patch_count, 2, head_count, head_size)  23.8 us
    ppermute x8, starting transfers between devices, passed_along(): return lax.ppermute(block, axis, route)  23.1 us
    dot_general x2, matrix products, attend_back(): jnp.einsum('bhqk,bqhe->bkhe', score_grad, queries, precision=lax.Precisio...  20.3 us
    another operation x2, local copies, waits for them, and re-layouts, encode_back(): kv_grad = jnp.stack([key_grad, value_grad], 2)  13.4 us
    convert_element_type x2, local copies, waits for them, and re-layouts, encode_back(): kv_grad = jnp.transpose(kv_grad, (1, 0, 2, 3, 4)).reshape(level_total * p...  12.4 us
    dot_general x2, matrix products, attend(): jnp.einsum('bqhe,bkhe->bhqk', queries, key_part, precision=lax.Precision....  10.3 us
    ppermute x8, waiting for transfers between devices, passed_along(): return lax.ppermute(block, axis, route)  9.66 us
  transfers between devices with their start and end apart: 9, of which 3 were waited for; matrix products, arithmetic and copies ran while one was open for 35% of the time, Pallas kernels for 0%

commit v1 on v0

v1 whole, which is shorter than its diff:
```python
import math

import jax
import jax.numpy as jnp
from jax import lax
from jax.experimental import pallas as pl
from jax.experimental.pallas import tpu as pltpu
from jax.sharding import PartitionSpec as P

MESH = pl.DeviceIdType.MESH
BF = jnp.bfloat16
F32 = jnp.float32

D = 512
HEADS = 16
HD = 32
LEVELS = 13
WLAT = 6
WLON = 12
PADC = 16
PATCH = WLAT * PADC
TOK = 2 * WLAT * WLON
HALF = WLAT * WLON
EDGE = 128
GRP = 8
GW = GRP * HD
GT = GRP * TOK
EPS = 1e-05
NEG = -1e30
GRAD_GAIN = 6.0
SCALE = 1.0 / math.sqrt(HD)

NY, NX, NZ = 4, 4, 8
WIDE = 1024
QW = 768
OW = 256

(
    C_GE, C_GN, C_EE, C_EN, C_AW, C_AS, C_XW, C_XS,
    C_TN, C_TR, C_TC, C_TQ,
) = range(12)
C_O1A = 12
C_O1B = 15
C_Q1A = 18
C_Q1B = 21
C_2A = 24
C_2B = 27
C_3A = 30
C_3B = 37
N_COPY = 44


def nt(a, b):
    return lax.dot_general(a, b, (((1,), (1,)), ((), ())), preferred_element_type=F32)


def nn(a, b):
    return lax.dot_general(a, b, (((1,), (0,)), ((), ())), preferred_element_type=F32)


def iota(shape, dim):
    return lax.broadcasted_iota(jnp.int32, shape, dim)


def split_token(t):
    level = (t >= HALF).astype(jnp.int32)
    rest = t - HALF * level
    row = lax.shift_right_logical(rest * 171, 11)
    return level, row, rest - row * WLON


def split_edge(u):
    level = (u >= 60).astype(jnp.int32)
    rest = u - 60 * level
    row = lax.shift_right_logical(rest * 171, 11)
    return level, row, rest - row * WLON


def one_hot(index, keep, width):
    shape = (index.shape[0], width)
    return jnp.where(keep & (index == iota(shape, 1)), 1.0, 0.0).astype(BF)


def padded(block):
    lead = block.shape[0]
    full = jnp.concatenate([block, jnp.zeros((lead, PADC - WLON, D), block.dtype)], 1)
    return full.reshape(lead * PADC, D)


def lanes_of(values, shape, dim, step):
    index = iota(shape, dim)
    out = jnp.zeros(shape, F32)
    for k, v in enumerate(values):
        out = jnp.where((index >= k * step) & (index < (k + 1) * step), v, out)
    return out


def kernel(
    lev_hbm, q_ref, kvw_hbm, eo_hbm, etemp_ref, wq_hbm, wo_hbm, stemp_ref, lats_ref, lons_ref, valid_ref, og_ref,
    out_ref, lg_ref, gq_ref, go_ref,
    lev, kvw, eo, wq, wo,
    levp, vals, prob, wexp, prod, vgrad, encp, score,
    own_e, re_e, sn_e, rn_e, own_g, re_g, sn_g, rn_g,
    att, rw_a, ss_a, rs_a, xg, rw_x, ss_x, rs_x,
    unit, qkv, normed, rgrad, ctx, qgrad,
    m_normed, m_rgrad, m_ctx, m_qgrad,
    qs, cgs, pt, p16, bias, hmask, fold,
    send_a, send_b, r1a, r1b, s2a, s2b, r2a, r2b, s3a, s3b, r3a, r3b,
    lsem, ssem, rsem,
):
    lat = lax.axis_index("lat")
    lon = lax.axis_index("lon")
    y_hi = lat // 8
    x = (lat // 2) % 4
    core = lat % 2
    z = lon // 2
    y_lo = lon % 2
    y = y_hi * 2 + y_lo

    def device(yy, xx, cc, zz):
        return ((yy // 2) * 8 + xx * 2 + cc, zz * 2 + yy % 2)

    mate = (lat + 1 - 2 * core, lon)
    east = (lat, (lon + 1) % 16)
    west = (lat, (lon + 15) % 16)
    north = ((lat + 1) % 16, lon)
    south = ((lat + 15) % 16, lon)
    y_peers = [device((y + k) % NY, x, core, z) for k in range(1, NY)]
    x_peers = [device(y, (x + k) % NX, core, z) for k in range(1, NX)]
    z_peers = [device(y, x, core, (z + k) % NZ) for k in range(1, NZ)]
    greeted = [mate, east, west, north, south] + y_peers + x_peers + z_peers
    barrier = pltpu.get_barrier_semaphore()
    for peer in greeted:
        pl.semaphore_signal(barrier, inc=1, device_id=peer, device_id_type=MESH)

    loads = [
        pltpu.make_async_copy(src, dst, lsem.at[i])
        for i, (src, dst) in enumerate(
            [(kvw_hbm, kvw), (lev_hbm, lev), (eo_hbm, eo), (wq_hbm, wq), (wo_hbm, wo)]
        )
    ]
    for load in loads:
        load.start()

    started = []

    def send(src, dst, index, peer):
        copy = pltpu.make_async_remote_copy(
            src_ref=src, dst_ref=dst, send_sem=ssem.at[index], recv_sem=rsem.at[index],
            device_id=peer, device_id_type=MESH,
        )
        copy.start()
        started.append(copy)
        return copy

    s = lats_ref[0]
    t = lons_ref[0]

    tok = iota((TOK, 1), 0)
    lv, ri, cj = split_token(tok)
    i2 = ri + s
    j2 = cj + t
    in_n = i2 >= WLAT
    in_e = j2 >= WLON
    base = lv * HALF + i2 * WLON + j2
    sel_own = one_hot(base, (~in_n) & (~in_e), TOK)
    sel_e = one_hot(base - WLON, (~in_n) & in_e, TOK)
    sel_n = one_hot(lv * 60 + (i2 - WLAT) * WLON + cj, in_n, EDGE)
    edge = iota((EDGE, 1), 0)
    elv, er, ec = split_edge(edge)
    real = edge < 120
    ej = ec + t
    ebase = elv * HALF + er * WLON + ej
    edge_own = one_hot(ebase, real & (ej < WLON), TOK)
    edge_e = one_hot(ebase - WLON, real & (ej >= WLON), TOK)
    compact = one_hot((lv * WLAT + ri) * PADC + cj, tok >= 0, 2 * PATCH)

    own_g[...] = nn(compact, jnp.concatenate([padded(og_ref[0]), padded(og_ref[1])], 0)).astype(BF)
    pl.semaphore_wait(barrier, len(greeted))
    ge = send(own_g, re_g, C_GE, west)

    q_rows = jnp.concatenate([jnp.broadcast_to(q_ref[l : l + 1, :], (HEADS, D)) for l in range(2)], 0)
    row_head = iota((2 * HEADS, D), 0) % HEADS
    lane_head = lax.shift_right_logical(iota((2 * HEADS, D), 1), 5)
    q_rows = jnp.where(row_head == lane_head, q_rows.astype(F32), 0.0).astype(BF)
    enc_scale = [etemp_ref[h] * SCALE for h in range(HEADS)]
    loads[0].wait()
    key_q = nt(q_rows, kvw[:, :D])
    folded = key_q * lanes_of(enc_scale * 2, (2 * HEADS, 1), 0, 1)
    fold_hi = folded.astype(BF)
    fold_lo = (folded - fold_hi.astype(F32)).astype(BF)
    loads[1].wait()
    for m in range(LEVELS):
        levp[m * PATCH : (m + 1) * PATCH, :] = padded(lev[m])
    for m in range(LEVELS):
        rows = slice(m * PATCH, (m + 1) * PATCH)
        level = levp[rows, :]
        vals[rows, :] = nn(level, kvw[:, D:]).astype(BF)
        score[m] = nt(level, fold_hi) + nt(level, fold_lo)
    peak = score[0]
    for m in range(1, LEVELS):
        peak = jnp.maximum(peak, score[m])
    total = jnp.zeros_like(peak)
    for m in range(LEVELS):
        e = jnp.exp(score[m] - peak)
        score[m] = e
        total = total + e
    inverse = 1.0 / total
    spread_row = iota((2 * HEADS, 2 * D), 0)
    spread = jnp.where(lax.shift_right_logical(iota((2 * HEADS, 2 * D), 1), 5) == spread_row, 1.0, 0.0).astype(BF)
    for m in range(LEVELS):
        pm = score[m] * inverse
        prob[m] = pm
        wexp[m * PATCH : (m + 1) * PATCH, :] = nn(pm.astype(BF), spread).astype(BF)
    for r in range(WLAT):
        acc0 = jnp.zeros((PADC, D), F32)
        acc1 = jnp.zeros((PADC, D), F32)
        for m in range(LEVELS):
            rows = slice(m * PATCH + r * PADC, m * PATCH + (r + 1) * PADC)
            v = vals[rows, :].astype(F32)
            acc0 = acc0 + wexp[rows, :D].astype(F32) * v
            acc1 = acc1 + wexp[rows, D:].astype(F32) * v
        encp[r * PADC : (r + 1) * PADC, :] = acc0.astype(BF)
        encp[PATCH + r * PADC : PATCH + (r + 1) * PADC, :] = acc1.astype(BF)
    loads[2].wait()
    mixed = nn(encp[...], eo[...])
    encoded = jnp.concatenate(
        [q_ref[l : l + 1, :].astype(F32) + mixed[l * PATCH : (l + 1) * PATCH, :] for l in range(2)], 0
    ).astype(BF)
    encp[...] = encoded
    own_e[...] = nn(compact, encoded).astype(BF)
    ee = send(own_e, re_e, C_EE, west)

    ge.wait_recv()
    sn_g[...] = (nn(edge_own, own_g[...]) + nn(edge_e, re_g[...])).astype(BF)
    gn = send(sn_g, rn_g, C_GN, south)
    tq = iota((1, GT), 1)
    for k in range(1, GRP):
        tq = jnp.where(iota((1, GT), 1) >= k * TOK, iota((1, GT), 1) - k * TOK, tq)
    qlv, qri, qcj = split_token(tq)
    first_wrapped = 96 - s
    wrap_k = (lat * WLAT + ri) >= first_wrapped
    wrap_q = (lat * WLAT + qri) >= first_wrapped
    lane = iota((TOK, WLON), 1)
    valid_row = jnp.zeros((TOK, WLON), jnp.int32)
    for r in range(WLAT):
        valid_row = jnp.where(ri == r, valid_ref[r : r + 1, :], valid_row)
    valid_k = jnp.sum(jnp.where(lane == cj, valid_row, 0), 1, keepdims=True)
    kk = iota((TOK, GT), 0)
    wk = jnp.where(wrap_k, 1, 0)
    wqv = jnp.where(wrap_q, 1, 0)
    ok = (wk == wqv) & ((valid_k == 1) | (kk == tq))
    bias[...] = jnp.where(ok, 0.0, NEG)
    fold[...] = jnp.where(kk == tq, 1.0, 0.0).astype(BF)
    fh = lax.shift_right_logical(iota((GW, GT), 0), 5)
    lane_t = iota((GW, GT), 1)
    hmask[...] = jnp.where((lane_t >= fh * TOK) & (lane_t < (fh + 1) * TOK), 1.0, 0.0).astype(BF)
    group_head = lax.shift_right_logical(iota((TOK, GW), 1), 5)
    eye = jnp.where(iota((GW, GW), 0) == iota((GW, GW), 1), 1.0, 0.0).astype(BF)
    scale_rows = [
        lanes_of([stemp_ref[g * GRP + h] * SCALE for h in range(GRP)], (1, GT), 1, TOK) for g in range(2)
    ]
    n = iota((256, 1), 0)
    bit = lambda shift, mask: lax.shift_right_logical(n, shift) & mask
    wrow = bit(7, 1) * 256 + bit(4, 3) * 64 + core * 32 + bit(1, 7) * 4 + bit(6, 1) * 2 + (n & 1)
    pick = one_hot(wrow, n >= 0, D)

    gn.wait_recv()
    rgrad[...] = (nn(sel_own, own_g[...]) + nn(sel_e, re_g[...]) + nn(sel_n, rn_g[...])).astype(BF)
    tr = send(rgrad, m_rgrad, C_TR, mate)
    loads[4].wait()
    cgrad = nt(rgrad[...], wo[...]).astype(BF)
    for g in range(2):
        part = cgrad[:, g * GW : (g + 1) * GW]
        for h in range(GRP):
            cgs[g, h * TOK : (h + 1) * TOK, :] = jnp.where(group_head == h, part, jnp.zeros_like(part))

    ee.wait_recv()
    sn_e[...] = (nn(edge_own, own_e[...]) + nn(edge_e, re_e[...])).astype(BF)
    en = send(sn_e, rn_e, C_EN, south)
    near = nn(sel_own, own_e[...]) + nn(sel_e, re_e[...])
    en.wait_recv()
    rolled = near + nn(sel_n, rn_e[...])

    mean = jnp.mean(rolled, 1, keepdims=True)
    centered = rolled - mean
    inv = lax.rsqrt(jnp.mean(centered * centered, 1, keepdims=True) + EPS)
    unit_v = centered * inv
    unit[...] = unit_v
    normed[...] = unit_v.astype(BF)
    tn = send(normed, m_normed, C_TN, mate)
    loads[3].wait()
    qkv[...] = nn(normed[...], wq[...]).astype(BF)
    for g in range(2):
        lanes = slice(g * GW, (g + 1) * GW)
        qg = qkv[:, g * GW : (g + 1) * GW]
        for h in range(GRP):
            qs[g, h * TOK : (h + 1) * TOK, :] = jnp.where(group_head == h, qg, jnp.zeros_like(qg))
        st = nt(qkv[:, D + g * GW : D + (g + 1) * GW], qs[g]) * scale_rows[g] + bias[...]
        e = jnp.exp(st - jnp.max(st, 0, keepdims=True))
        p = e * (1.0 / jnp.sum(e, 0, keepdims=True))
        pt[g] = p
        p16[g] = p.astype(BF)
        v_t = nt(eye, qkv[:, 2 * D + g * GW : 2 * D + (g + 1) * GW]).astype(BF)
        c_t = nn(v_t, p16[g]).astype(BF) * hmask[...]
        ctx[:, lanes] = nt(fold[...], c_t).astype(BF)
    tc = send(ctx, m_ctx, C_TC, mate)
    att[...] = nn(ctx[...], wo[...]).astype(BF)
    aw = send(att, rw_a, C_AW, east)

    for g in range(2):
        lanes = slice(g * GW, (g + 1) * GW)
        p = pt[g]
        dp = nt(qkv[:, 2 * D + g * GW : 2 * D + (g + 1) * GW], cgs[g])
        ds = p * (dp - jnp.sum(p * dp, 0, keepdims=True)) * scale_rows[g]
        ds16 = ds.astype(BF)
        kg = qkv[:, D + g * GW : D + (g + 1) * GW]
        k_t = nt(eye, kg).astype(BF)
        q_t = nn(k_t, ds16).astype(BF) * hmask[...]
        qgrad[:, lanes] = nt(fold[...], q_t).astype(BF)
        qgrad[:, D + g * GW : D + (g + 1) * GW] = nn(ds16, qs[g]).astype(BF)
        qgrad[:, 2 * D + g * GW : 2 * D + (g + 1) * GW] = nn(p16[g], cgs[g]).astype(BF)
    tqc = send(qgrad, m_qgrad, C_TQ, mate)

    ugrad = nt(qgrad[...], wq[...])
    u = unit[...]
    xgrad = inv * (
        ugrad - jnp.mean(ugrad, 1, keepdims=True) - u * jnp.mean(ugrad * u, 1, keepdims=True)
    )
    xg[...] = xgrad.astype(BF)
    xw = send(xg, rw_x, C_XW, east)

    bl, br, bc = elv, er + 1, ec
    back_j = bc - t
    bbase = bl * HALF + br * WLON + back_j
    bedge_own = one_hot(bbase, real & (back_j >= 0), TOK)
    bedge_w = one_hot(bbase + WLON, real & (back_j < 0), TOK)
    pp = iota((2 * PATCH, 1), 0)
    pl_ = (pp >= PATCH).astype(jnp.int32)
    prest = pp - PATCH * pl_
    pr = lax.shift_right_logical(prest, 4)
    pc = prest & 15
    inside = pc < WLON
    ii = pr - s
    jj = pc - t
    pbase = pl_ * HALF + ii * WLON + jj
    pad_own = one_hot(pbase, inside & (ii >= 0) & (jj >= 0), TOK)
    pad_w = one_hot(pbase + WLON, inside & (ii >= 0) & (jj < 0), TOK)
    pad_s = one_hot(pl_ * 60 + (ii + WLAT - 1) * WLON + pc, inside & (ii < 0), EDGE)

    aw.wait_recv()
    ss_a[...] = (nn(bedge_own, att[...]) + nn(bedge_w, rw_a[...])).astype(BF)
    as_ = send(ss_a, rs_a, C_AS, north)

    def chip_sum(left, m_left, right, m_right):
        mine = nt(pick, left[...]).astype(BF)
        other = nt(pick, m_left[...]).astype(BF)
        return nn(mine, right[...]) + nn(other, m_right[...])

    def share(width, low, slab_a, slab_b, first_a, first_b):
        for k in range(1, NY):
            src = send_a.at[(y + k) % NY, :, :, pl.ds(low, width)]
            slab_a.append(send(src, r1a.at[k - 1, :, :, pl.ds(low, width)], first_a + k - 1, y_peers[k - 1]))
        for k in range(1, NX):
            src = send_b.at[:, (x + k) % NX, :, pl.ds(low, width)]
            slab_b.append(send(src, r1b.at[k - 1, :, :, pl.ds(low, width)], first_b + k - 1, x_peers[k - 1]))

    first_stage = []
    tc.wait_recv()
    tr.wait_recv()
    g_out = chip_sum(ctx, m_ctx, rgrad, m_rgrad).astype(BF).reshape(NY, NX, 16, D)
    send_a[:, :, :, QW:] = g_out[:, :, :, :OW]
    send_b[:, :, :, QW:] = g_out[:, :, :, OW:]
    share(OW, QW, first_stage, first_stage, C_O1A, C_O1B)
    tn.wait_recv()
    tqc.wait_recv()
    g_qkv = chip_sum(normed, m_normed, qgrad, m_qgrad).astype(BF).reshape(NY, NX, 16, 3 * D)
    send_a[:, :, :, :QW] = g_qkv[:, :, :, :QW]
    send_b[:, :, :, :QW] = g_qkv[:, :, :, QW:]
    share(QW, 0, first_stage, first_stage, C_Q1A, C_Q1B)

    xw.wait_recv()
    ss_x[...] = (nn(bedge_own, xg[...]) + nn(bedge_w, rw_x[...])).astype(BF)
    xs = send(ss_x, rs_x, C_XS, north)
    as_.wait_recv()
    back_a = nn(pad_own, att[...]) + nn(pad_w, rw_a[...]) + nn(pad_s, rs_a[...])
    out16 = (encp[...].astype(F32) + back_a).astype(BF)
    out_ref[...] = out16.reshape(2, WLAT, PADC, D)[:, :, :WLON, :]
    xs.wait_recv()
    back_x = nn(pad_own, xg[...]) + nn(pad_w, rw_x[...]) + nn(pad_s, rs_x[...])
    og_pad = jnp.concatenate([padded(og_ref[0]), padded(og_ref[1])], 0)
    egrad = (og_pad.astype(F32) + back_x).astype(BF)

    encp[...] = nt(egrad, eo[...]).astype(BF)

    def products(r):
        c0 = encp[r * PADC : (r + 1) * PADC, :].astype(F32)
        c1 = encp[PATCH + r * PADC : PATCH + (r + 1) * PADC, :].astype(F32)
        for m in range(LEVELS):
            rows = slice(m * PATCH + r * PADC, m * PATCH + (r + 1) * PADC)
            v = vals[rows, :].astype(F32)
            prod[rows, :D] = (c0 * v).astype(BF)
            prod[rows, D:] = (c1 * v).astype(BF)
            vgrad[rows, :] = (wexp[rows, :D].astype(F32) * c0 + wexp[rows, D:].astype(F32) * c1).astype(BF)

    for r in range(WLAT):
        products(r)

    for copy in first_stage:
        copy.wait_recv()
    sum_a = send_a[y].astype(F32)
    sum_b = send_b[:, x].astype(F32)
    for k in range(3):
        sum_a = sum_a + r1a[k].astype(F32)
        sum_b = sum_b + r1b[k].astype(F32)
    s2a[...] = sum_a.astype(BF)
    s2b[...] = sum_b.astype(BF)
    second_stage = []
    for k in range(1, NX):
        second_stage.append(send(s2a.at[(x + k) % NX], r2a.at[k - 1], C_2A + k - 1, x_peers[k - 1]))
    for k in range(1, NY):
        second_stage.append(send(s2b.at[(y + k) % NY], r2b.at[k - 1], C_2B + k - 1, y_peers[k - 1]))

    sums = jnp.zeros((PATCH, 2 * HEADS), F32)
    for m in range(LEVELS):
        pg = nt(prod[m * PATCH : (m + 1) * PATCH, :], spread)
        score[m] = pg
        sums = sums + prob[m] * pg
    lane_scale = lanes_of(enc_scale * 2, (1, 2 * HEADS), 1, 1)

    for copy in second_stage:
        copy.wait_recv()
    last_a = s2a[x].astype(F32)
    last_b = s2b[y].astype(F32)
    for k in range(3):
        last_a = last_a + r2a[k].astype(F32)
        last_b = last_b + r2b[k].astype(F32)
    for k in range(NZ):
        s3a[k] = last_a[2 * k : 2 * k + 2, :]
        s3b[k] = last_b[2 * k : 2 * k + 2, :]
    third_stage = []
    for k in range(1, NZ):
        third_stage.append(send(s3a.at[(z + k) % NZ], r3a.at[k - 1], C_3A + k - 1, z_peers[k - 1]))
        third_stage.append(send(s3b.at[(z + k) % NZ], r3b.at[k - 1], C_3B + k - 1, z_peers[k - 1]))

    key_q16 = key_q.astype(BF)
    for m in range(LEVELS):
        rows = slice(m * PATCH, (m + 1) * PATCH)
        sg = prob[m] * (score[m] - sums) * lane_scale
        lg = nt(vgrad[rows, :], kvw[:, D:]) + nn(sg.astype(BF), key_q16)
        lg_ref[m] = lg.astype(BF).reshape(WLAT, PADC, D)[:, :WLON, :]

    for copy in third_stage:
        copy.wait_recv()
    fin_a = s3a[z]
    fin_b = s3b[z]
    for k in range(NZ - 1):
        fin_a = fin_a + r3a[k]
        fin_b = fin_b + r3b[k]
    factor = GRAD_GAIN * (2 * 96 * 192) ** (-0.5)
    gq_ref[:, :QW] = fin_a[:, :QW] * factor
    gq_ref[:, QW:] = fin_b[:, :QW] * factor
    go_ref[:, :OW] = fin_a[:, QW:] * factor
    go_ref[:, OW:] = fin_b[:, QW:] * factor
    for copy in started:
        copy.wait_send()


def local(levels_in, latent_queries, enc_kv, enc_out, enc_temp, w_qkv, w_out, swin_temp, lat_shift, lon_shift, key_valid, output_grad):
    vmem = pl.BlockSpec(memory_space=pltpu.VMEM)
    smem = pl.BlockSpec(memory_space=pltpu.SMEM)
    hbm = pl.BlockSpec(memory_space=pl.ANY)
    V = pltpu.VMEM
    block = lambda rows: V((rows, D), BF)
    scratch = [
        V((LEVELS, WLAT, WLON, D), BF), V((D, 2 * D), BF), V((D, D), BF), V((D, 3 * D), BF), V((D, D), BF),
        V((LEVELS * PATCH, D), BF),
        V((LEVELS * PATCH, D), BF),
        V((LEVELS, PATCH, 2 * HEADS), F32),
        V((LEVELS * PATCH, 2 * D), BF),
        V((LEVELS * PATCH, 2 * D), BF),
        V((LEVELS * PATCH, D), BF),
        block(2 * PATCH),
        V((LEVELS, PATCH, 2 * HEADS), F32),
        block(TOK), block(TOK), block(EDGE), block(EDGE),
        block(TOK), block(TOK), block(EDGE), block(EDGE),
        block(TOK), block(TOK), block(EDGE), block(EDGE),
        block(TOK), block(TOK), block(EDGE), block(EDGE),
        V((TOK, D), F32), V((TOK, 3 * D), BF), block(TOK), block(TOK), block(TOK), V((TOK, 3 * D), BF),
        block(TOK), block(TOK), block(TOK), V((TOK, 3 * D), BF),
        V((2, GT, GW), BF), V((2, GT, GW), BF), V((2, TOK, GT), F32), V((2, TOK, GT), BF),
        V((TOK, GT), F32), V((GW, GT), BF), V((TOK, GT), BF),
        V((NY, NX, 16, WIDE), BF), V((NY, NX, 16, WIDE), BF),
        V((3, NX, 16, WIDE), BF), V((3, NY, 16, WIDE), BF),
        V((NX, 16, WIDE), BF), V((NY, 16, WIDE), BF),
        V((3, 16, WIDE), BF), V((3, 16, WIDE), BF),
        V((NZ, 2, WIDE), F32), V((NZ, 2, WIDE), F32),
        V((NZ - 1, 2, WIDE), F32), V((NZ - 1, 2, WIDE), F32),
        pltpu.SemaphoreType.DMA((5,)),
        pltpu.SemaphoreType.DMA((N_COPY,)),
        pltpu.SemaphoreType.DMA((N_COPY,)),
    ]
    out, lg, gq, go = pl.pallas_call(
        kernel,
        out_shape=(
            jax.ShapeDtypeStruct((2, WLAT, WLON, D), BF),
            jax.ShapeDtypeStruct((LEVELS, WLAT, WLON, D), BF),
            jax.ShapeDtypeStruct((2, 3 * D), F32),
            jax.ShapeDtypeStruct((2, D), F32),
        ),
        in_specs=[hbm, vmem, hbm, hbm, smem, hbm, hbm, smem, smem, smem, vmem, vmem],
        out_specs=(vmem, vmem, vmem, vmem),
        scratch_shapes=scratch,
        compiler_params=pltpu.CompilerParams(
            collective_id=0, has_side_effects=True, vmem_limit_bytes=56 * 1024 * 1024
        ),
    )(levels_in, latent_queries, enc_kv, enc_out, enc_temp, w_qkv, w_out, swin_temp, lat_shift, lon_shift, key_valid, output_grad)
    return out, lg, gq.reshape(-1), go.reshape(-1)


def solution(mesh):
    return jax.shard_map(
        local,
        mesh=mesh,
        in_specs=(
            P(None, "lat", "lon", None), P(), P(), P(), P(), P(), P(), P(), P(), P(),
            P("lat", "lon"),
            P(None, "lat", "lon", None),
        ),
        out_specs=(
            P(None, "lat", "lon", None),
            P(None, "lat", "lon", None),
            P(("lat", "lon")),
            P(("lat", "lon")),
        ),
        check_vma=False,
    )
```

time: 404 us -> 71.6 us (0.18)
  waiting for transfers between devices: 204 us -> 0 us
  local copies, waits for them, and re-layouts: 79.2 us -> 11.7 us
  matrix products: 58.7 us -> 0 us
  Pallas kernels: 0 us -> 57.6 us
  starting transfers between devices: 23.1 us -> 0 us
  other arithmetic: 18.9 us -> 0 us
  between operations: 16.5 us -> 1.93 us
    unnamed x2 -> x0, waiting for transfers between devices: 194 us -> none
    dot_general x21 -> x0, matrix products: 58.7 us -> none  [the longest x2 20.3 us: attend_back(): jnp.einsum('bhqk,bqhe->bkhe', score_grad, queries, precision=lax.Precisio...]
    pallas_call x0 -> x1, Pallas kernels: none -> 57.6 us  [local(): pl.pallas_call(kernel, out_shape=(jax.ShapeDtypeStruct((2, WLAT, WLON, D)...]
    reshape x8 -> x1, local copies, waits for them, and re-layouts: 31.5 us -> 1.32 us  [local(): return (out, lg, gq.reshape(-1), go.reshape(-1))]
    ppermute x8 -> x0, starting transfers between devices: 23.1 us -> none  [passed_along(): return lax.ppermute(block, axis, route)]
    convert_element_type x7 -> x0, local copies, waits for them, and re-layouts: 18.9 us -> none  [the longest x2 12.4 us: encode_back(): kv_grad = jnp.transpose(kv_grad, (1, 0, 2, 3, 4)).reshape(level_total * p...]
    another operation x5 -> x0, local copies, waits for them, and re-layouts: 13.5 us -> none  [the longest x2 13.4 us: encode_back(): kv_grad = jnp.stack([key_grad, value_grad], 2)]
    ppermute x8 -> x0, waiting for transfers between devices: 9.66 us -> none  [passed_along(): return lax.ppermute(block, axis, route)]
  transfers between devices with their start and end apart: 9 -> 0, of which waited for: 3 -> 0; matrix products, arithmetic and copies ran while one was open for 35% -> 0% of each run, Pallas kernels for 0% -> 0%
where the time goes in v1:
time: 71.6 us; the launch traced here: 71.2 us
  Pallas kernels  57.6 us (80%)
  local copies, waits for them, and re-layouts  11.7 us (16%)
  between operations  1.93 us (3%)
    pallas_call x1, Pallas kernels, local(): pl.pallas_call(kernel, out_shape=(jax.ShapeDtypeStruct((2, WLAT, WLON, D)...  57.6 us
    unnamed x5, local copies, waits for them, and re-layouts  10.4 us

profile of v1, /device:TPU:16, one launch (start us, length us, event | category | flops | bytes accessed | tf_op | source)
XLA Modules:
  0.0 71.2 jit_solution(2639394920047289961)
XLA Ops:
  1.9 1.6 %copy.17.og_ref = bf16[2,6,12,512]{3,2,1,0:T(8,128)(2,1)} copy(bf16[2,6,12,512]{3,0,2,1:T(2,128)(2,1)} %param.23) | data formatting | bytes 294912 | tf_op args[11]
  3.5 2.9 %copy.16.lev_hbm = bf16[13,6,12,512]{3,2,1,0:T(8,128)(2,1)} copy(bf16[13,6,12,512]{3,0,2,1:T(8,128)(2,1)} %param.12) | data formatting | bytes 1916928 | tf_op args[0]
  6.4 57.6 %shard_map.147 = (bf16[2,6,12,512]{3,2,1,0:T(8,128)(2,1)}, bf16[13,6,12,512]{3,2,1,0:T(8,128)(2,1)}, f32[2,1536]{1,0:T(2,128)}, f32[2,512]{1,0:T(2,128)}) custom-call(bf16[13,6,12,512]{3,2,1,0:T(8,128)(2,1)} %copy.16.lev_hbm, bf16[2,512]{1,0:T(2,128)(2,1)} %q_ref.1, bf16[512,1024]{1,0:T(8,128)(2,1)} %kvw_hbm.1, bf16[512,512]{1,0:T(8,128)(2,1)} %eo_hbm.1, ...), custom_call_target="tpu_custom_call" | custom-call | tf_op jit(solution)/shard_map/pallas_call | solution.py:503
  64.0 1.7 %copy.18 = bf16[2,6,12,512]{3,0,2,1:T(2,128)(2,1)} copy(bf16[2,6,12,512]{3,2,1,0:T(8,128)(2,1)} %get-tuple-element.12) | data formatting | bytes 294912
  65.8 1.3 %copy.20 = f32[1,4,2,128]{3,1,2,0:T(4,128)} copy(f32[1,4,2,128]{3,2,1,0:T(2,128)} %bitcast.3) | data formatting | bytes 8192
  67.0 1.3 %reshape.14 = f32[3072]{0:T(1024)} reshape(f32[2,1536]{1,0:T(2,128)} %get-tuple-element.10) | data formatting | bytes 24576 | tf_op jit(solution)/shard_map/reshape | solution.py:518
  68.4 2.9 %copy.19 = bf16[13,6,12,512]{3,0,2,1:T(8,128)(2,1)} copy(bf16[13,6,12,512]{3,2,1,0:T(8,128)(2,1)} %get-tuple-element.13) | data formatting | bytes 1916928

commit v2 on v1

v2 whole, which is shorter than its diff:
```python
import functools
import math

import jax
import jax.numpy as jnp
from jax import lax
from jax.experimental import pallas as pl
from jax.experimental.pallas import tpu as pltpu
from jax.sharding import PartitionSpec as P

MESH = pl.DeviceIdType.MESH
BF = jnp.bfloat16
F32 = jnp.float32

D = 512
HEADS = 16
HD = 32
LEVELS = 13
WLAT = 6
WLON = 12
PADL = 16
TOK = 2 * WLAT * WLON
HALF = WLAT * WLON
ROWS = HALF * PADL
CHUNK = 384
GRP = 8
GW = GRP * HD
GT = GRP * TOK
EPS = 1e-05
NEG = -1e30
GRAD_GAIN = 6.0
SCALE = 1.0 / math.sqrt(HD)

NY, NX, NZ = 4, 4, 8
WIDE = 1024
EARLY = 512
SIDE = 80
PAIR = 2 * SIDE

C_GE, C_EE, C_AW, C_XW, C_TN, C_TR, C_TC, C_TV, C_TQ0, C_TQ1 = range(10)
C_GN, C_EN, C_AS, C_XS = range(10, 18, 2)
C_E1A, C_E1B, C_M1A, C_M1B, C_L1A, C_L1B, C_2A, C_2B = range(18, 42, 3)
C_3 = 42
N_COPY = 49


def nt(a, b):
    return lax.dot_general(a, b, (((1,), (1,)), ((), ())), preferred_element_type=F32)


def nn(a, b):
    return lax.dot_general(a, b, (((1,), (0,)), ((), ())), preferred_element_type=F32)


def iota(shape, dim):
    return lax.broadcasted_iota(jnp.int32, shape, dim)


def split_token(t):
    level = (t >= HALF).astype(jnp.int32)
    rest = t - HALF * level
    row = lax.shift_right_logical(rest * 171, 11)
    return level, row, rest - row * WLON


def split_side(u, width):
    half = (u >= SIDE).astype(jnp.int32)
    rest = u - SIDE * half
    real = rest < HALF
    level = (rest >= HALF // 2).astype(jnp.int32)
    rest = rest - HALF // 2 * level
    row = lax.shift_right_logical(rest * 171, 11) if width == WLON else lax.shift_right_logical(rest * 43, 8)
    return half, level, row, rest - row * width, real


def one_hot(index, keep, width):
    shape = (index.shape[0], width)
    return jnp.where(keep & (index == iota(shape, 1)), 1.0, 0.0).astype(BF)


def roll_matrices(row_step, col_step, from_east):
    lv, ri, cj = split_token(iota((TOK, 1), 0))
    half, elv, er, ec, real = split_side(iota((PAIR, 1), 0), WLON)

    def along_lon(level, row, col, keep):
        inside = (col >= 0) & (col < WLON)
        own = one_hot(level * HALF + row * WLON + col, keep & inside, TOK)
        start = level * (HALF // 2) + row * (WLON // 2)
        side = start + col + (-WLON if from_east else WLON // 2)
        return own, one_hot(side, keep & (~inside), SIDE)

    row = ri + row_step
    here = (row >= 0) & (row < WLAT)
    own, side = along_lon(lv, row, cj + col_step, here)
    start = lv * (HALF // 2) + cj
    over = jnp.where(row >= WLAT, start + (row - WLAT) * WLON, SIDE + start + (row + 3) * WLON)
    far = one_hot(over, ~here, PAIR)
    edge_own, edge_side = along_lon(elv, er + 3 * half, ec + col_step, real)
    return own, side, far, edge_own, edge_side


def lanes_of(values, shape, dim, step):
    index = iota(shape, dim)
    out = jnp.zeros(shape, F32)
    for k, v in enumerate(values):
        out = jnp.where((index >= k * step) & (index < (k + 1) * step), v, out)
    return out


def kernel(
    late_col,
    lev_hbm, q_ref, kvw_hbm, eo_hbm, etemp_ref, wq_hbm, wo_hbm, stemp_ref, lats_ref, lons_ref, valid_ref, og_hbm,
    out_ref, lg_ref, gq_ref, go_ref,
    lev, kvw, eo, wq, wo, og,
    levp, vals, prob, wexp, prod, vgrad, part, cback, rows_f, kvp, out_v, lg_v,
    own_e, pk_e, rl_e, sn_e, rn_e,
    own_g, pk_g, rl_g, sn_g, rn_g,
    att, pk_a, rl_a, sn_a, rn_a,
    xg, pk_x, rl_x, sn_x, rn_x,
    unit, qkv, normed, rgrad, ctx, vback, qback,
    m_normed, m_rgrad, m_ctx, m_vback, m_qback,
    qs, cgs, pt, p16, bias, hmask, fold,
    send_a, send_b, r1a, r1b, s2a, s2b, r2a, r2b, s3f, s3, r3,
    lsem, ssem, rsem,
):
    lat = lax.axis_index("lat")
    lon = lax.axis_index("lon")
    y_hi = lat // 8
    x = (lat // 2) % 4
    core = lat % 2
    z = lon // 2
    y_lo = lon % 2
    y = y_hi * 2 + y_lo

    def device(yy, xx, cc, zz):
        return ((yy // 2) * 8 + xx * 2 + cc, zz * 2 + yy % 2)

    mate = (lat + 1 - 2 * core, lon)
    east = (lat, (lon + 1) % 16)
    west = (lat, (lon + 15) % 16)
    north = ((lat + 1) % 16, lon)
    south = ((lat + 15) % 16, lon)
    y_peers = [device((y + k) % NY, x, core, z) for k in range(1, NY)]
    x_peers = [device(y, (x + k) % NX, core, z) for k in range(1, NX)]
    z_peers = [device(y, x, core, (z + k) % NZ) for k in range(1, NZ)]
    greeted = [mate, east, west, north, south] + y_peers + x_peers + z_peers
    barrier = pltpu.get_barrier_semaphore()
    for peer in greeted:
        pl.semaphore_signal(barrier, inc=1, device_id=peer, device_id_type=MESH)

    loads = [
        pltpu.make_async_copy(src, dst, lsem.at[i])
        for i, (src, dst) in enumerate(
            [(kvw_hbm, kvw), (lev_hbm, lev), (eo_hbm, eo), (wq_hbm, wq), (wo_hbm, wo), (og_hbm, og)]
        )
    ]
    for i in (5, 0, 1, 2, 3, 4):
        loads[i].start()

    started = []

    def send(src, dst, index, peer):
        copy = pltpu.make_async_remote_copy(
            src_ref=src, dst_ref=dst, send_sem=ssem.at[index], recv_sem=rsem.at[index],
            device_id=peer, device_id_type=MESH,
        )
        copy.start()
        started.append(copy)
        return copy

    def send_pair(src, dst, index, first, second):
        halves = [pl.ds(0, SIDE), pl.ds(SIDE, SIDE)]
        return [
            send(src.at[h], dst.at[h], index + i, peer) for i, (h, peer) in enumerate(zip(halves, (first, second)))
        ]

    def arrived(copies):
        for copy in copies:
            copy.wait_recv()

    s = lats_ref[0]
    t = lons_ref[0]
    late_row = s > WLAT // 2
    row_step = jnp.where(late_row, s - WLAT, s)
    col_step = t - WLON if late_col else t
    ahead, back = (east, west) if late_col else (west, east)

    q_rows = jnp.concatenate([jnp.broadcast_to(q_ref[l : l + 1, :], (HEADS, D)) for l in range(2)], 0)
    row_head = iota((2 * HEADS, D), 0) % HEADS
    lane_head = lax.shift_right_logical(iota((2 * HEADS, D), 1), 5)
    q_rows = jnp.where(row_head == lane_head, q_rows.astype(F32), 0.0).astype(BF)
    lane_scale = lanes_of([etemp_ref[h] * SCALE for h in range(HEADS)] * 2, (1, 2 * HEADS), 1, 1)
    loads[0].wait()
    loads[1].wait()
    filler = jnp.zeros((8, PADL - LEVELS, D), BF)
    for c in range(HALF // 8):
        block = jnp.concatenate([lev[8 * c : 8 * c + 8], filler], 1)
        levp[8 * PADL * c : 8 * PADL * (c + 1), :] = block.reshape(8 * PADL, D)
    real_level = iota((CHUNK // PADL, PADL, 2 * HEADS), 1) < LEVELS
    for c in range(ROWS // CHUNK):
        rows = slice(c * CHUNK, (c + 1) * CHUNK)
        kv = nn(levp[rows, :], kvw[...])
        vals[rows, :] = kv[:, D:].astype(BF)
        sc = (nt(kv[:, :D].astype(BF), q_rows) * lane_scale).reshape(CHUNK // PADL, PADL, 2 * HEADS)
        sc = jnp.where(real_level, sc, NEG)
        e = jnp.exp(sc - jnp.max(sc, 1, keepdims=True))
        pm = e * (1.0 / jnp.sum(e, 1, keepdims=True))
        prob[rows, :] = pm.reshape(CHUNK, 2 * HEADS)
    spread_row = iota((2 * HEADS, 2 * D), 0)
    spread = jnp.where(lax.shift_right_logical(iota((2 * HEADS, 2 * D), 1), 5) == spread_row, 1.0, 0.0).astype(BF)
    for c in range(HALF // 8):
        rows = slice(8 * PADL * c, 8 * PADL * (c + 1))
        w = nn(prob[rows, :].astype(BF), spread)
        wexp[rows, :] = w.astype(BF)
        v = vals[rows, :].astype(F32)
        for l in range(2):
            product = (w[:, l * D : (l + 1) * D] * v).reshape(8, 2, 8, D)
            product = (product[:, 0] + product[:, 1]).reshape(64, D)
            for j in range(4):
                part[4 * l + j, 64 * c : 64 * (c + 1), :] = product[:, 128 * j : 128 * (j + 1)]
        for l in range(2):
            for j in range(4):
                acc = part[4 * l + j, pl.ds(64 * c, 8, stride=8), :]
                for m in range(1, 8):
                    acc = acc + part[4 * l + j, pl.ds(64 * c + m, 8, stride=8), :]
                cback[l * HALF + 8 * c : l * HALF + 8 * (c + 1), 128 * j : 128 * (j + 1)] = acc
    loads[2].wait()
    mixed = nn(cback[...].astype(BF), eo[...])
    token_level = iota((TOK, D), 0) >= HALF
    query = jnp.where(token_level, q_ref[1:2, :].astype(F32), q_ref[0:1, :].astype(F32))
    enc16 = (query + mixed).astype(BF)
    own_e[...] = enc16
    _, plv, pr, pc, preal = split_side(iota((SIDE, 1), 0), WLON // 2)
    packs = [one_hot(plv * HALF + pr * WLON + pc + half * (WLON // 2), preal, TOK) for half in range(2)]
    pack_ahead, pack_back = packs[::-1] if late_col else packs
    kvp[...] = jnp.zeros((8, D), F32)
    kvp[0:WLAT, 0:WLON] = valid_ref[...].astype(F32)

    def with_valid(pair, valid_rows):
        return jnp.concatenate([pair[: pair.shape[0] - 8], valid_rows], 0).astype(BF)

    def valid_of(message):
        return message[message.shape[0] - 8 :, :].astype(F32)

    pk_e[...] = with_valid(nn(pack_ahead, enc16), kvp[...])
    pl.semaphore_wait(barrier, len(greeted))
    ee = send(pk_e, rl_e, C_EE, ahead)

    tok = iota((TOK, 1), 0)
    lv, ri, cj = split_token(tok)
    apart = one_hot((ri * WLON + cj) * 2 + lv, tok >= 0, TOK)
    loads[5].wait()
    for p in range(HALF):
        rows_f[2 * p : 2 * p + 2, :] = og[p].astype(F32)
    own_g[...] = nn(apart, rows_f[...].astype(BF)).astype(BF)
    pk_g[...] = nn(pack_ahead, own_g[...]).astype(BF)
    ge = send(pk_g, rl_g, C_GE, ahead)

    sel_own, sel_side, sel_far, edge_own, edge_side = roll_matrices(row_step, col_step, not late_col)
    edge_near = nn(edge_own, own_e[...])
    near = nn(sel_own, own_e[...])
    tq = iota((1, GT), 1)
    for k in range(1, GRP):
        tq = jnp.where(iota((1, GT), 1) >= k * TOK, iota((1, GT), 1) - k * TOK, tq)
    qri = split_token(tq)[1]
    first_wrapped = 16 * WLAT - s
    window_row = jnp.where(late_row, (lat + 15) % 16, lat) * WLAT
    wk = jnp.where(window_row + ri >= first_wrapped, 1, 0)
    wqv = jnp.where(window_row + qri >= first_wrapped, 1, 0)
    kk = iota((TOK, GT), 0)
    fold[...] = jnp.where(kk == tq, 1.0, 0.0).astype(BF)
    fh = lax.shift_right_logical(iota((GW, GT), 0), 5)
    lane_t = iota((GW, GT), 1)
    hmask[...] = jnp.where((lane_t >= fh * TOK) & (lane_t < (fh + 1) * TOK), 1.0, 0.0).astype(BF)
    group_head = lax.shift_right_logical(iota((TOK, GW), 1), 5)
    eye = jnp.where(iota((GW, GW), 0) == iota((GW, GW), 1), 1.0, 0.0).astype(BF)
    scale_rows = [
        lanes_of([stemp_ref[g * GRP + h] * SCALE for h in range(GRP)], (1, GT), 1, TOK) for g in range(2)
    ]
    n = iota((256, 1), 0)
    bit = lambda shift, mask: lax.shift_right_logical(n, shift) & mask
    wrow = bit(7, 1) * 256 + bit(4, 3) * 64 + core * 32 + bit(1, 7) * 4 + bit(6, 1) * 2 + (n & 1)
    pick = one_hot(wrow, n >= 0, D)

    ee.wait_recv()
    valid_1 = valid_of(rl_e) if late_col else kvp[...]
    sn_e[...] = with_valid(edge_near + nn(edge_side, rl_e[...]), valid_1)
    en = send_pair(sn_e, rn_e, C_EN, south, north)
    near = near + nn(sel_side, rl_e[...])
    ge.wait_recv()
    sn_g[...] = (nn(edge_own, own_g[...]) + nn(edge_side, rl_g[...])).astype(BF)
    gn = send_pair(sn_g, rn_g, C_GN, south, north)
    near_g = nn(sel_own, own_g[...]) + nn(sel_side, rl_g[...])
    back_own, back_side, back_far, bedge_own, bedge_side = roll_matrices(-row_step, -col_step, late_col)
    loads[3].wait()
    loads[4].wait()
    arrived(en)
    valid_2 = jnp.where(late_row, valid_of(rn_e), valid_1)
    lane = iota((TOK, 128), 1)
    valid_row = jnp.zeros((TOK, 128), F32)
    for r in range(WLAT):
        valid_row = jnp.where(ri == r, valid_2[r : r + 1, :128], valid_row)
    valid_k = jnp.sum(jnp.where(lane == cj, valid_row, 0.0), 1, keepdims=True)
    ok = (wk == wqv) & ((valid_k > 0.5) | (kk == tq))
    bias[...] = jnp.where(ok, 0.0, NEG)
    rolled = near + nn(sel_far, rn_e[...])

    mean = jnp.mean(rolled, 1, keepdims=True)
    centered = rolled - mean
    inv = lax.rsqrt(jnp.mean(centered * centered, 1, keepdims=True) + EPS)
    unit_v = centered * inv
    unit[...] = unit_v
    normed[...] = unit_v.astype(BF)
    tn = send(normed, m_normed, C_TN, mate)
    qkv[...] = nn(normed[...], wq[...]).astype(BF)
    for g in range(2):
        lanes = slice(g * GW, (g + 1) * GW)
        qg = qkv[:, g * GW : (g + 1) * GW]
        for h in range(GRP):
            qs[g, h * TOK : (h + 1) * TOK, :] = jnp.where(group_head == h, qg, jnp.zeros_like(qg))
        st = nt(qkv[:, D + g * GW : D + (g + 1) * GW], qs[g]) * scale_rows[g] + bias[...]
        e = jnp.exp(st - jnp.max(st, 0, keepdims=True))
        p = e * (1.0 / jnp.sum(e, 0, keepdims=True))
        pt[g] = p
        p16[g] = p.astype(BF)
        v_t = nt(eye, qkv[:, 2 * D + g * GW : 2 * D + (g + 1) * GW]).astype(BF)
        c_t = nn(v_t, p16[g]).astype(BF) * hmask[...]
        ctx[:, lanes] = nt(fold[...], c_t).astype(BF)
    tc = send(ctx, m_ctx, C_TC, mate)
    att[...] = nn(ctx[...], wo[...]).astype(BF)
    pk_a[...] = nn(pack_back, att[...]).astype(BF)
    aw = send(pk_a, rl_a, C_AW, back)

    arrived(gn)
    rgrad[...] = (near_g + nn(sel_far, rn_g[...])).astype(BF)
    tr = send(rgrad, m_rgrad, C_TR, mate)
    cgrad = nt(rgrad[...], wo[...]).astype(BF)
    for g in range(2):
        piece = cgrad[:, g * GW : (g + 1) * GW]
        for h in range(GRP):
            cgs[g, h * TOK : (h + 1) * TOK, :] = jnp.where(group_head == h, piece, jnp.zeros_like(piece))

    for g in range(2):
        vback[:, g * GW : (g + 1) * GW] = nn(p16[g], cgs[g]).astype(BF)
    tv = send(vback, m_vback, C_TV, mate)

    def scores_back(g):
        p = pt[g]
        dp = nt(qkv[:, 2 * D + g * GW : 2 * D + (g + 1) * GW], cgs[g])
        ds = p * (dp - jnp.sum(p * dp, 0, keepdims=True)) * scale_rows[g]
        ds16 = ds.astype(BF)
        k_t = nt(eye, qkv[:, D + g * GW : D + (g + 1) * GW]).astype(BF)
        q_t = nn(k_t, ds16).astype(BF) * hmask[...]
        qback[g, :, :GW] = nt(fold[...], q_t).astype(BF)
        qback[g, :, GW:] = nn(ds16, qs[g]).astype(BF)
        return send(qback.at[g], m_qback.at[g], C_TQ0 + g, mate)

    def picked(left, m_left):
        return nt(pick, left[...]).astype(BF), nt(pick, m_left[...]).astype(BF)

    def chip_sum(lefts, right, m_right):
        total = nn(lefts[0], right) + nn(lefts[1], m_right)
        return total.astype(BF).reshape(NY, NX, 16, right.shape[1])

    first_stage = []

    def share(low, width, first_a, first_b):
        lanes = pl.ds(low, width)
        for k in range(1, NY):
            src = send_a.at[(y + k) % NY, :, :, lanes]
            first_stage.append(send(src, r1a.at[k - 1, :, :, lanes], first_a + k - 1, y_peers[k - 1]))
        for k in range(1, NX):
            src = send_b.at[:, (x + k) % NX, :, lanes]
            first_stage.append(send(src, r1b.at[k - 1, :, :, lanes], first_b + k - 1, x_peers[k - 1]))

    tq0 = scores_back(0)
    tc.wait_recv()
    tr.wait_recv()
    g_out = chip_sum(picked(ctx, m_ctx), rgrad[...], m_rgrad[...])
    send_a[:, :, :, 768:] = g_out[:, :, :, :256]
    send_b[:, :, :, 768:] = g_out[:, :, :, 256:]
    tn.wait_recv()
    tv.wait_recv()
    lefts = picked(normed, m_normed)
    g_val = chip_sum(lefts, vback[...], m_vback[...])
    send_a[:, :, :, 512:768] = g_val[:, :, :, :256]
    send_b[:, :, :, 512:768] = g_val[:, :, :, 256:]
    share(512, 512, C_E1A, C_E1B)
    tq1 = scores_back(1)

    ugrad = nt(vback[...], wq[:, 2 * D :])
    for g in range(2):
        ugrad = ugrad + nt(qback[g, :, :GW], wq[:, g * GW : (g + 1) * GW])
        ugrad = ugrad + nt(qback[g, :, GW:], wq[:, D + g * GW : D + (g + 1) * GW])
    u = unit[...]
    xgrad = inv * (
        ugrad - jnp.mean(ugrad, 1, keepdims=True) - u * jnp.mean(ugrad * u, 1, keepdims=True)
    )
    xg[...] = xgrad.astype(BF)
    pk_x[...] = nn(pack_back, xg[...]).astype(BF)
    xw = send(pk_x, rl_x, C_XW, back)
    for g, copy, a1, b1 in ((0, tq0, C_M1A, C_M1B), (1, tq1, C_L1A, C_L1B)):
        copy.wait_recv()
        g_qk = chip_sum(lefts, qback[g], m_qback[g])
        send_a[:, :, :, g * GW : (g + 1) * GW] = g_qk[:, :, :, :GW]
        send_b[:, :, :, g * GW : (g + 1) * GW] = g_qk[:, :, :, GW:]
        share(g * GW, GW, a1, b1)
    near_x = own_g[...].astype(F32) + nn(back_own, xg[...])
    edge_x = nn(bedge_own, xg[...])
    aw.wait_recv()
    sn_a[...] = (nn(bedge_own, att[...]) + nn(bedge_side, rl_a[...])).astype(BF)
    near_a = nn(back_own, att[...]) + nn(back_side, rl_a[...])

    xw.wait_recv()
    sn_x[...] = (edge_x + nn(bedge_side, rl_x[...])).astype(BF)
    xs = send_pair(sn_x, rn_x, C_XS, south, north)
    near_x = near_x + nn(back_side, rl_x[...])
    as_ = send_pair(sn_a, rn_a, C_AS, south, north)
    for copy in first_stage:
        copy.wait_recv()
    sum_a = send_a[y].astype(F32)
    sum_b = send_b[:, x].astype(F32)
    for k in range(3):
        sum_a = sum_a + r1a[k].astype(F32)
        sum_b = sum_b + r1b[k].astype(F32)
    s2a[...] = sum_a.astype(BF)
    s2b[...] = sum_b.astype(BF)
    second_stage = []
    for k in range(1, NX):
        second_stage.append(send(s2a.at[(x + k) % NX], r2a.at[k - 1], C_2A + k - 1, x_peers[k - 1]))
    for k in range(1, NY):
        second_stage.append(send(s2b.at[(y + k) % NY], r2b.at[k - 1], C_2B + k - 1, y_peers[k - 1]))

    arrived(xs)
    egrad = (near_x + nn(back_far, rn_x[...])).astype(BF)

    cback[...] = nt(egrad, eo[...]).astype(BF).astype(F32)

    for p in range(HALF):
        rows = slice(p * PADL, (p + 1) * PADL)
        c0 = cback[p : p + 1, :]
        c1 = cback[HALF + p : HALF + p + 1, :]
        v = vals[rows, :].astype(F32)
        prod[rows, :D] = (c0 * v).astype(BF)
        prod[rows, D:] = (c1 * v).astype(BF)
        vgrad[rows, :] = (wexp[rows, :D].astype(F32) * c0 + wexp[rows, D:].astype(F32) * c1).astype(BF)

    key_q = nt(q_rows, kvw[:, :D]).astype(BF)
    for c in range(ROWS // CHUNK):
        rows = slice(c * CHUNK, (c + 1) * CHUNK)
        pg = nt(prod[rows, :], spread).reshape(CHUNK // PADL, PADL, 2 * HEADS)
        pm = prob[rows, :].reshape(CHUNK // PADL, PADL, 2 * HEADS)
        sg = pm * (pg - jnp.sum(pm * pg, 1, keepdims=True))
        prob[rows, :] = sg.reshape(CHUNK, 2 * HEADS) * lane_scale

    for copy in second_stage:
        copy.wait_recv()
    last_a = s2a[x].astype(F32)
    last_b = s2b[y].astype(F32)
    for k in range(3):
        last_a = last_a + r2a[k].astype(F32)
        last_b = last_b + r2b[k].astype(F32)
    for j in range(8):
        value = (last_a if j < 4 else last_b)[:, 256 * (j % 4) : 256 * (j % 4 + 1)]
        for h in range(2):
            s3f[h, pl.ds(j, 16, stride=8), :] = value[:, 128 * h : 128 * (h + 1)]
    for k in range(NZ):
        for h in range(2):
            s3[k, :, 128 * h : 128 * (h + 1)] = s3f[h, 16 * k : 16 * (k + 1), :].astype(BF)
    third_stage = []
    for k in range(1, NZ):
        third_stage.append(send(s3.at[(z + k) % NZ], r3.at[k - 1], C_3 + k - 1, z_peers[k - 1]))

    stores = []
    for c in range(ROWS // CHUNK):
        rows = slice(c * CHUNK, (c + 1) * CHUNK)
        lg = nt(vgrad[rows, :], kvw[:, D:]) + nn(prob[rows, :].astype(BF), key_q)
        patches = slice(c * CHUNK // PADL, (c + 1) * CHUNK // PADL)
        lg_v[patches] = lg.astype(BF).reshape(CHUNK // PADL, PADL, D)[:, :LEVELS, :]
        stores.append(pltpu.make_async_copy(lg_v.at[patches], lg_ref.at[patches], lsem.at[6 + c]))
        stores[-1].start()

    arrived(as_)
    out16 = (own_e[...].astype(F32) + (near_a + nn(back_far, rn_a[...]))).astype(BF)
    u_row = iota((TOK, 1), 0)
    together = one_hot((u_row & 1) * HALF + lax.shift_right_logical(u_row, 1), u_row >= 0, TOK)
    rows_f[...] = nn(together, out16)
    for p in range(HALF):
        out_v[p] = rows_f[2 * p : 2 * p + 2, :].astype(BF)
    stores.append(pltpu.make_async_copy(out_v, out_ref, lsem.at[9]))
    stores[-1].start()

    for copy in third_stage:
        copy.wait_recv()
    factor = GRAD_GAIN * (2 * 96 * 192) ** (-0.5)
    for h in range(2):
        total = s3f[h, pl.ds(pl.multiple_of(16 * z, 16), 16), :]
        for k in range(NZ - 1):
            total = total + r3[k, :, 128 * h : 128 * (h + 1)].astype(F32)
        total = total * factor
        for b in range(2):
            for j, row in ((0, 0), (1, 2), (4, 4), (5, 6), (2, 8), (6, 10)):
                at = 12 * b + row + h
                gq_ref[at : at + 1, :] = total[8 * b + j : 8 * b + j + 1, :]
            for j, row in ((3, 0), (7, 2)):
                at = 4 * b + row + h
                go_ref[at : at + 1, :] = total[8 * b + j : 8 * b + j + 1, :]
    for copy in started:
        copy.wait_send()
    for copy in stores:
        copy.wait()


def deliver(a, b, c, d, a_out, b_out, c_out, d_out, sems):
    pairs = ((a, a_out), (b, b_out), (c, c_out), (d, d_out))
    copies = [pltpu.make_async_copy(src, dst, sems.at[i]) for i, (src, dst) in enumerate(pairs)]
    for copy in copies:
        copy.start()
    for copy in copies:
        copy.wait()


def local(levels_in, latent_queries, enc_kv, enc_out, enc_temp, w_qkv, w_out, swin_temp, lat_shift, lon_shift, key_valid, output_grad):
    vmem = pl.BlockSpec(memory_space=pltpu.VMEM)
    smem = pl.BlockSpec(memory_space=pltpu.SMEM)
    hbm = pl.BlockSpec(memory_space=pl.ANY)
    V = pltpu.VMEM
    block = lambda rows: V((rows, D), BF)
    scratch = [
        V((HALF, LEVELS, D), BF), V((D, 2 * D), BF), V((D, D), BF), V((D, 3 * D), BF), V((D, D), BF), V((HALF, 2, D), BF),
        V((ROWS, D), BF),
        V((ROWS, D), BF),
        V((ROWS, 2 * HEADS), F32),
        V((ROWS, 2 * D), BF),
        V((ROWS, 2 * D), BF),
        V((ROWS, D), BF),
        V((8, 8 * HALF, 128), F32),
        V((TOK, D), F32),
        V((TOK, D), F32),
        V((8, D), F32),
        V((HALF, 2, D), BF),
        V((HALF, LEVELS, D), BF),
    ]
    for _ in range(4):
        scratch += [block(TOK), block(SIDE), block(SIDE), block(PAIR), block(PAIR)]
    scratch += [
        V((TOK, D), F32), V((TOK, 3 * D), BF), block(TOK), block(TOK), block(TOK), block(TOK), V((2, TOK, D), BF),
        block(TOK), block(TOK), block(TOK), block(TOK), V((2, TOK, D), BF),
        V((2, GT, GW), BF), V((2, GT, GW), BF), V((2, TOK, GT), F32), V((2, TOK, GT), BF),
        V((TOK, GT), F32), V((GW, GT), BF), V((TOK, GT), BF),
        V((NY, NX, 16, WIDE), BF), V((NY, NX, 16, WIDE), BF),
        V((3, NX, 16, WIDE), BF), V((3, NY, 16, WIDE), BF),
        V((NX, 16, WIDE), BF), V((NY, 16, WIDE), BF),
        V((3, 16, WIDE), BF), V((3, 16, WIDE), BF),
        V((2, 128, 128), F32), V((NZ, 16, 256), BF), V((NZ - 1, 16, 256), BF),
        pltpu.SemaphoreType.DMA((10,)),
        pltpu.SemaphoreType.DMA((N_COPY,)),
        pltpu.SemaphoreType.DMA((N_COPY,)),
    ]
    lev = jnp.transpose(levels_in, (1, 2, 0, 3)).reshape(HALF, LEVELS, D)
    og = jnp.transpose(output_grad, (1, 2, 0, 3)).reshape(HALF, 2, D)
    shapes = (
        jax.ShapeDtypeStruct((HALF, 2, D), BF),
        jax.ShapeDtypeStruct((HALF, LEVELS, D), BF),
        jax.ShapeDtypeStruct((24, 128), F32),
        jax.ShapeDtypeStruct((8, 128), F32),
    )

    def run(late_col):
        return pl.pallas_call(
            functools.partial(kernel, late_col),
            out_shape=shapes,
            in_specs=[hbm, vmem, hbm, hbm, smem, hbm, hbm, smem, smem, smem, vmem, hbm],
            out_specs=(hbm, hbm, vmem, vmem),
            scratch_shapes=scratch,
            compiler_params=pltpu.CompilerParams(
                collective_id=int(late_col), has_side_effects=True, vmem_limit_bytes=48 * 1024 * 1024
            ),
        )

    parts = lax.cond(
        lon_shift[0] > WLON // 2, run(True), run(False),
        lev, latent_queries, enc_kv, enc_out, enc_temp, w_qkv, w_out, swin_temp, lat_shift, lon_shift, key_valid, og,
    )
    out, lg, gq, go = pl.pallas_call(
        deliver,
        out_shape=shapes,
        in_specs=[hbm] * 4,
        out_specs=(hbm,) * 4,
        scratch_shapes=[pltpu.SemaphoreType.DMA((4,))],
    )(*parts)
    out = jnp.transpose(out.reshape(WLAT, WLON, 2, D), (2, 0, 1, 3))
    lg = jnp.transpose(lg.reshape(WLAT, WLON, LEVELS, D), (2, 0, 1, 3))
    return out, lg, gq.reshape(-1), go.reshape(-1)


def solution(mesh):
    return jax.shard_map(
        local,
        mesh=mesh,
        in_specs=(
            P(None, "lat", "lon", None), P(), P(), P(), P(), P(), P(), P(), P(), P(),
            P("lat", "lon"),
            P(None, "lat", "lon", None),
        ),
        out_specs=(
            P(None, "lat", "lon", None),
            P(None, "lat", "lon", None),
            P(("lat", "lon")),
            P(("lat", "lon")),
        ),
        check_vma=False,
    )
```

time: 71.6 us -> 52.4 us (0.73)
  local copies, waits for them, and re-layouts: 11.7 us -> 0 us
  Pallas kernels: 57.6 us -> 49.9 us
    unnamed x5 -> x0, local copies, waits for them, and re-layouts: 10.4 us -> none
    pallas_call x1 -> x2, Pallas kernels: 57.6 us -> 49.9 us  [the longest x1 48.8 us: local(): lax.cond(lon_shift[0] > WLON // 2, run(True), run(False), lev, latent_que...]
    reshape x1 -> x0, local copies, waits for them, and re-layouts: 1.32 us -> none  [local(): return (out, lg, gq.reshape(-1), go.reshape(-1))]
where the time goes in v2:
time: 52.4 us; the launch traced here: 51.5 us
  Pallas kernels  49.9 us (95%)
  between operations  1.45 us (3%)
    pallas_call x1, Pallas kernels, local(): lax.cond(lon_shift[0] > WLON // 2, run(True), run(False), lev, latent_que...  48.8 us
    pallas_call x1, Pallas kernels, local(): pl.pallas_call(deliver, out_shape=shapes, in_specs=[hbm] * 4, out_specs=(...  1.1 us

profile of v2, /device:TPU:16, one launch (start us, length us, event | category | flops | bytes accessed | tf_op | source)
XLA Modules:
  0.0 51.5 jit_solution(5138142734205624055)
XLA Ops:
  1.3 49.0 %conditional.1 = ((bf16[72,2,512]{2,1,0:T(2,128)(2,1)S(1)}, bf16[72,13,512]{2,1,0:T(8,128)(2,1)S(1)}, f32[24,128]{1,0:T(8,128)S(1)}, f32[8,128]{1,0:T(8,128)S(1)})) conditional(s32[]{:T(128)} %bitcast, (bf16[72,13,512]{2,1,0:T(8,128)(2,1)}, bf16[2,512]{1,0:T(2,128)(2,1)}, bf16[512,1024]{1,0:T(8,128)(2,1)}, bf16[512,512]{1,0:T(8,128)(2,1)}, ...), branch_computations={%region_0.0_spmd, %region_1.0_spmd} | conditional | bytes 8 | solution.py:581
  1.5 48.8 %branch_1_fun.1 = (bf16[72,2,512]{2,1,0:T(2,128)(2,1)S(1)}, bf16[72,13,512]{2,1,0:T(8,128)(2,1)S(1)}, f32[24,128]{1,0:T(8,128)S(1)}, f32[8,128]{1,0:T(8,128)S(1)}) custom-call(bf16[72,13,512]{2,1,0:T(8,128)(2,1)} %get-tuple-element.60.lev_hbm, bf16[2,512]{1,0:T(2,128)(2,1)} %get-tuple-element.61.q_ref, bf16[512,1024]{1,0:T(8,128)(2,1)} %get-tuple-element.62.kvw_hbm, ...), custom_call_target="tpu_custom_call" | custom-call | tf_op jit(solution)/shard_map/cond/branch_1_fun/pallas_call | solution.py:581
  50.2 1.1 %shard_map.147 = (bf16[72,2,512]{2,1,0:T(2,128)(2,1)}, bf16[72,13,512]{2,1,0:T(8,128)(2,1)}, f32[24,128]{1,0:T(8,128)}, f32[8,128]{1,0:T(8,128)}) custom-call(bf16[72,2,512]{2,1,0:T(2,128)(2,1)S(1)} %get-tuple-element.84.a, bf16[72,13,512]{2,1,0:T(8,128)(2,1)S(1)} %get-tuple-element.85.b, f32[24,128]{1,0:T(8,128)S(1)} %get-tuple-element.86.c, ...), custom_call_target="tpu_custom_call" | custom-call | tf_op jit(solution)/shard_map/pallas_call | solution.py:585

commit v3 on v2

v3 whole, which is shorter than its diff:
```python
import functools
import math

import jax
import jax.numpy as jnp
from jax import lax
from jax.experimental import pallas as pl
from jax.experimental.pallas import tpu as pltpu
from jax.sharding import PartitionSpec as P

MESH = pl.DeviceIdType.MESH
BF = jnp.bfloat16
F32 = jnp.float32

D = 512
HEADS = 16
HD = 32
LEVELS = 13
WLAT = 6
WLON = 12
PADL = 16
TOK = 2 * WLAT * WLON
HALF = WLAT * WLON
ROWS = HALF * PADL
CHUNK = 384
GRP = 8
GW = GRP * HD
GT = GRP * TOK
EPS = 1e-05
NEG = -1e30
GRAD_GAIN = 6.0
SCALE = 1.0 / math.sqrt(HD)

NY, NX, NZ = 4, 4, 8
WIDE = 1024
PIECES = ((0, 1, 2, 8, 9, 10, 12, 13), (4, 5, 3, 6, 7, 11, 14, 15))
EDGES = (0, 80, 128, 160, 240, 304)
PLACES = tuple(zip(EDGES[:-1], EDGES[1:]))
LON_AT, THREE_DIAG, TWO_DIAG, THREE_AT, TWO_AT, SIDES = EDGES
SIDES_1 = 160
FIRST = 40

(
    C_EE, C_GE, C_AW, C_XW, C_TN, C_TR, C_TC, C_TV, C_TQ0, C_TQ1, C_GN, C_AS, C_XS, C_1A, C_1B, C_2A, C_2B, C_3,
) = range(18)
N_COPY = 18
THREE, BOTH = 80, 144


def nt(a, b):
    return lax.dot_general(a, b, (((1,), (1,)), ((), ())), preferred_element_type=F32)


def nn(a, b):
    return lax.dot_general(a, b, (((1,), (0,)), ((), ())), preferred_element_type=F32)


def iota(shape, dim):
    return lax.broadcasted_iota(jnp.int32, shape, dim)


def split_token(t):
    level = (t >= HALF).astype(jnp.int32)
    rest = t - HALF * level
    row = lax.shift_right_logical(rest * 171, 11)
    return level, row, rest - row * WLON


def block_index(level, row, col, late_col):
    half = (col >= 6).astype(jnp.int32)
    return level * HALF + (1 - half if late_col else half) * 36 + row * 6 + col - 6 * half


def split_block(t, late_col):
    level = (t >= HALF).astype(jnp.int32)
    rest = t - HALF * level
    second = (rest >= 36).astype(jnp.int32)
    rest = rest - 36 * second
    row = lax.shift_right_logical(rest * 43, 8)
    return level, row, rest - 6 * row + 6 * (1 - second if late_col else second)


def window_index(level, row, col):
    return level * HALF + row * WLON + col


def split_part(u, rows, cols):
    size = rows * cols
    level = (u >= size).astype(jnp.int32)
    rest = u - size * level
    row = lax.shift_right_logical(rest * 171, 11) if cols == WLON else lax.shift_right_logical(rest * 43, 8)
    return level, row, rest - row * cols, u < 2 * size


def one_hot(index, keep, width):
    shape = (index.shape[0], width)
    return jnp.where(keep & (index == iota(shape, 1)), 1.0, 0.0).astype(BF)


def lon_pack(last_cols):
    level, row, col, real = split_part(iota((THREE, 1), 0), WLAT, 6)
    return one_hot(window_index(level, row, col + 6 * last_cols), real, TOK)


def block_packs(late_col):
    shapes = ((WLAT, 6, 0), (3, 6, 0), (2, 6, 4), (3, WLON, 0), (2, WLON, 4))
    first, rest = [], []
    for k, ((at, end), (rows, cols, r0)) in enumerate(zip(PLACES, shapes)):
        level, row, col, real = split_part(iota((end - at, 1), 0), rows, cols)
        if k < 3:
            first.append(one_hot(level * FIRST + (row + r0) * 6 + col, real, 2 * FIRST))
        else:
            rest.append(one_hot(block_index(level, row + r0, col, late_col), real, TOK))
    return jnp.concatenate(first, 0), jnp.concatenate(rest, 0)


def roll_matrices(row_step, col_step, last_cols):
    lv, ri, cj = split_token(iota((TOK, 1), 0))
    row, col = ri + row_step, cj + col_step
    row_in = (row >= 0) & (row < WLAT)
    col_in = (col >= 0) & (col < WLON)
    own = one_hot(block_index(lv, row, col, last_cols), row_in & col_in, TOK)
    far_col = col + (WLON // 2 if last_cols else -WLON)
    over = row >= WLAT
    far_row = jnp.where(over, row - WLAT, row + 2)
    line = far_row * WLON + col
    corner = far_row * 6 + far_col
    lon = LON_AT + lv * 36 + row * 6 + far_col
    lat = jnp.where(over, THREE_AT + lv * 36 + line, TWO_AT + lv * 24 + line)
    diag = jnp.where(over, THREE_DIAG + lv * 18 + corner, TWO_DIAG + lv * 12 + corner)
    side = jnp.where(row_in, lon, jnp.where(col_in, lat, diag))
    return own, one_hot(side, ~(row_in & col_in), SIDES)


def two_step_matrices(row_step, col_step, three_last, last_cols, place, index):
    def along_lon(level, row, col, keep):
        inside = (col >= 0) & (col < WLON)
        own = one_hot(index(level, row, col), keep & inside, TOK)
        far_col = col + (WLON // 2 if last_cols else -WLON)
        return own, one_hot(level * 36 + row * 6 + far_col, keep & (~inside), THREE)

    lv, ri, cj = place(iota((TOK, 1), 0))
    row = ri + row_step
    row_in = (row >= 0) & (row < WLAT)
    own, side = along_lon(lv, row, cj + col_step, row_in)
    over = row >= WLAT
    line = jnp.where(over, row - WLAT, row + (3 if three_last else 2)) * WLON + cj
    in_three = ~over if three_last else over
    far = one_hot(jnp.where(in_three, lv * 36 + line, THREE + lv * 24 + line), ~row_in, BOTH)
    edges = []
    for length, rows, first in ((THREE, 3, 3 if three_last else 0), (BOTH - THREE, 2, 0 if three_last else 4)):
        level, row, col, real = split_part(iota((length, 1), 0), rows, WLON)
        edges.append(along_lon(level, row + first, col + col_step, real))
    edge_own, edge_side = (jnp.concatenate([e[i] for e in edges], 0) for i in range(2))
    return own, side, far, edge_own, edge_side


def lanes_of(values, shape, dim, step):
    index = iota(shape, dim)
    out = jnp.zeros(shape, F32)
    for k, v in enumerate(values):
        out = jnp.where((index >= k * step) & (index < (k + 1) * step), v, out)
    return out


def kernel(
    late_col,
    lev_hbm, q_hbm, kvw_hbm, eo_hbm, etemp_hbm, wq_hbm, wo_hbm, stemp_hbm, lats_hbm, lons_hbm, valid_hbm, og_hbm,
    out_hbm, lg_hbm, gq_hbm, go_hbm,
    lev, kvw, eo, wq, wo, og, q_ref, etemp_ref, stemp_ref, lats_ref, lons_ref, valid_ref,
    levp, vals, prob, wexp, prod, vgrad, part, cback, rows_f, kvp, out_v, lg_v, gq_ref, go_ref,
    own_e, pk_e, rl_e,
    own_g, pk_g, rl_g, sn_g, rn_g,
    att, pk_a, rl_a, sn_a, rn_a,
    xg, pk_x, rl_x, sn_x, rn_x,
    unit, qkv, normed, rgrad, ctx, qgrad,
    m_normed, m_rgrad, m_ctx, m_qgrad,
    qs, cgs, pt, p16, bias, hmask, fold,
    send_a, send_b, r1a, r1b, s2a, s2b, r2a, r2b, s3f, s3, r3,
    lsem, ssem, rsem,
):
    lat = lax.axis_index("lat")
    lon = lax.axis_index("lon")
    y_hi = lat // 8
    x = (lat // 2) % 4
    core = lat % 2
    z = lon // 2
    y_lo = lon % 2
    y = y_hi * 2 + y_lo

    def device(yy, xx, cc, zz):
        return ((yy // 2) * 8 + xx * 2 + cc, zz * 2 + yy % 2)

    mate = (lat + 1 - 2 * core, lon)
    east = (lat, (lon + 1) % 16)
    west = (lat, (lon + 15) % 16)
    north = ((lat + 1) % 16, lon)
    south = ((lat + 15) % 16, lon)
    y_peers = [device((y + k) % NY, x, core, z) for k in range(1, NY)]
    x_peers = [device(y, (x + k) % NX, core, z) for k in range(1, NX)]
    z_peers = [device(y, x, core, (z + k) % NZ) for k in range(1, NZ)]
    lon_ahead, lon_back = (east, west) if late_col else (west, east)
    ahead = (lon_ahead, (south[0], lon_ahead[1]), (north[0], lon_ahead[1]), south, north)
    greeted = [mate, *ahead, lon_back, (north[0], lon_back[1]), (south[0], lon_back[1])] + y_peers + x_peers + z_peers
    barrier = pltpu.get_barrier_semaphore()
    for peer in greeted:
        pl.semaphore_signal(barrier, inc=1, device_id=peer, device_id_type=MESH)

    loads = []

    def load(src, dst):
        loads.append(pltpu.make_async_copy(src, dst, lsem.at[len(loads)]))
        loads[-1].start()
        return loads[-1]

    small = [
        load(src, dst)
        for src, dst in (
            (lats_hbm, lats_ref), (lons_hbm, lons_ref), (valid_hbm, valid_ref), (q_hbm, q_ref),
            (etemp_hbm, etemp_ref), (stemp_hbm, stemp_ref),
        )
    ]
    load_og = load(og_hbm, og)
    load_kvw = load(kvw_hbm, kvw)
    load_lev = load(lev_hbm, lev)
    landings = {}

    def send(src, dst, index, peer, landing=None):
        landings[index] = dst if landing is None else landing
        pltpu.make_async_remote_copy(
            src_ref=src, dst_ref=dst, send_sem=ssem.at[index], recv_sem=rsem.at[index],
            device_id=peer, device_id_type=MESH,
        ).start()

    def whole(index):
        return pltpu.make_async_remote_copy(
            src_ref=landings[index], dst_ref=landings[index], send_sem=ssem.at[index], recv_sem=rsem.at[index],
            device_id=mate, device_id_type=MESH,
        )

    def arrived(index):
        whole(index).wait_recv()

    def send_sides(places, peers):
        for (at, end), peer in zip(places, peers):
            part_of = pl.ds(at, end - at)
            send(pk_e.at[part_of], rl_e.at[part_of], C_EE, peer, rl_e)

    def send_lat(src, dst, index, three_to, two_to):
        for part_of, peer in ((pl.ds(0, THREE), three_to), (pl.ds(THREE, BOTH - THREE), two_to)):
            send(src.at[part_of], dst.at[part_of], index, peer, dst)

    pack_first, pack_rest = block_packs(late_col)
    pack_back = lon_pack(not late_col)
    tok = iota((TOK, 1), 0)
    lv, ri, cj = split_token(tok)
    own_index = functools.partial(block_index, late_col=late_col)
    own_place = functools.partial(split_block, late_col=late_col)
    olv, ori, ocj = own_place(tok)
    apart = one_hot((ori * WLON + ocj) * 2 + olv, tok >= 0, TOK)
    load_og.wait()
    for p in range(HALF):
        rows_f[2 * p : 2 * p + 2, :] = og[p].astype(F32)
    own_g[...] = nn(apart, rows_f[...].astype(BF)).astype(BF)
    glv, gri, gcj, greal = split_part(iota((THREE, 1), 0), WLAT, 6)
    pk_g[...] = nn(one_hot(glv * HALF + gri * 6 + gcj, greal, TOK), own_g[...]).astype(BF)
    pl.semaphore_wait(barrier, len(greeted))
    send(pk_g, rl_g, C_GE, lon_ahead)
    for copy in small:
        copy.wait()
    s = lats_ref[0]
    t = lons_ref[0]
    late_row = s > WLAT // 2
    row_step = jnp.where(late_row, s - WLAT, s)
    col_step = t - WLON if late_col else t
    sel_own, sel_side = roll_matrices(row_step, col_step, late_col)
    kvp[...] = jnp.zeros((8, D), F32)
    kvp[0:WLAT, 0:WLON] = valid_ref[...].astype(F32)

    def with_valid(sides, places):
        pieces, base = [], places[0][0]
        for at, end in places:
            pieces += [sides[at - base : end - base - 8], kvp[...]]
        return jnp.concatenate(pieces, 0).astype(BF)

    q_rows = jnp.concatenate([jnp.broadcast_to(q_ref[l : l + 1, :], (HEADS, D)) for l in range(2)], 0)
    row_head = iota((2 * HEADS, D), 0) % HEADS
    lane_head = lax.shift_right_logical(iota((2 * HEADS, D), 1), 5)
    q_rows = jnp.where(row_head == lane_head, q_rows.astype(F32), 0.0).astype(BF)
    lane_scale = lanes_of([etemp_ref[h] * SCALE for h in range(HEADS)] * 2, (1, 2 * HEADS), 1, 1)
    load_kvw.wait()
    load_lev.wait()
    load_eo = load(eo_hbm, eo)
    load_wo = load(wo_hbm, wo)
    wq_sem = lsem.at[len(loads)]
    for src, dst, width in ((0, 0, GW), (D, GW, GW), (GW, D, GW), (D + GW, D + GW, GW), (2 * D, 2 * D, D)):
        pltpu.make_async_copy(wq_hbm.at[:, pl.ds(src, width)], wq.at[:, pl.ds(dst, width)], wq_sem).start()
    filler = jnp.zeros((6, PADL - LEVELS, D), BF)

    def run_of(k):
        return 12 * (k % WLAT) + 6 * ((k // WLAT) ^ int(late_col))

    for k in range(2 * WLAT):
        block = jnp.concatenate([lev[run_of(k) : run_of(k) + 6], filler], 1)
        levp[6 * PADL * k : 6 * PADL * (k + 1), :] = block.reshape(6 * PADL, D)
    spread_row = iota((2 * HEADS, 2 * D), 0)
    spread = jnp.where(lax.shift_right_logical(iota((2 * HEADS, 2 * D), 1), 5) == spread_row, 1.0, 0.0).astype(BF)

    def encode_rows(low, high):
        rows, count = slice(low, high), (high - low) // PADL
        kv = nn(levp[rows, :], kvw[...])
        vals[rows, :] = kv[:, D:].astype(BF)
        sc = (nt(kv[:, :D].astype(BF), q_rows) * lane_scale).reshape(count, PADL, 2 * HEADS)
        sc = jnp.where(iota((count, PADL, 2 * HEADS), 1) < LEVELS, sc, NEG)
        e = jnp.exp(sc - jnp.max(sc, 1, keepdims=True))
        pm = e * (1.0 / jnp.sum(e, 1, keepdims=True))
        prob[rows, :] = pm.reshape(high - low, 2 * HEADS)

    def context_of(c):
        rows = slice(8 * PADL * c, 8 * PADL * (c + 1))
        w = nn(prob[rows, :].astype(BF), spread)
        wexp[rows, :] = w.astype(BF)
        v = vals[rows, :].astype(F32)
        for l in range(2):
            product = (w[:, l * D : (l + 1) * D] * v).reshape(8, 2, 8, D)
            product = (product[:, 0] + product[:, 1]).reshape(64, D)
            for j in range(4):
                part[4 * l + j, 64 * c : 64 * (c + 1), :] = product[:, 128 * j : 128 * (j + 1)]
        for l in range(2):
            for j in range(4):
                acc = part[4 * l + j, pl.ds(64 * c, 8, stride=8), :]
                for m in range(1, 8):
                    acc = acc + part[4 * l + j, pl.ds(64 * c + m, 8, stride=8), :]
                cback[l * HALF + 8 * c : l * HALF + 8 * (c + 1), 128 * j : 128 * (j + 1)] = acc

    def encoded_of(low, high):
        count = high - low
        context = jnp.concatenate([cback[low:high, :], cback[HALF + low : HALF + high, :]], 0)
        mixed = nn(context.astype(BF), eo[...])
        second = iota((2 * count, D), 0) >= count
        query = jnp.where(second, q_ref[1:2, :].astype(F32), q_ref[0:1, :].astype(F32))
        result = (query + mixed).astype(BF)
        for l in range(2):
            rows_f[l * HALF + low : l * HALF + high, :] = result[l * count : (l + 1) * count].astype(F32)
        return result

    encode_rows(0, 320)
    encode_rows(320, 640)
    for c in range(FIRST // 8):
        context_of(c)
    load_eo.wait()
    pk_e[:SIDES_1, :] = with_valid(nn(pack_first, encoded_of(0, FIRST)), PLACES[:3])
    send_sides(PLACES[:3], ahead[:3])
    encode_rows(640, 896)
    encode_rows(896, 1152)
    for c in range(FIRST // 8, HALF // 8):
        context_of(c)
    encoded_of(FIRST, HALF)
    own_e[...] = rows_f[...].astype(BF)
    pk_e[SIDES_1:, :] = with_valid(nn(pack_rest, own_e[...]), PLACES[3:])
    send_sides(PLACES[3:], ahead[3:])
    near = nn(sel_own, own_e[...])
    two_own, two_side, two_far, two_edge_own, two_edge_side = two_step_matrices(
        row_step, col_step, False, late_col, split_token, own_index
    )
    near_g = nn(two_own, own_g[...])
    edge_g = nn(two_edge_own, own_g[...])
    arrived(C_GE)
    sn_g[...] = (edge_g + nn(two_edge_side, rl_g[...])).astype(BF)
    send_lat(sn_g, rn_g, C_GN, south, north)
    near_g = near_g + nn(two_side, rl_g[...])
    tq = iota((1, GT), 1)
    for k in range(1, GRP):
        tq = jnp.where(iota((1, GT), 1) >= k * TOK, iota((1, GT), 1) - k * TOK, tq)
    qri = split_token(tq)[1]
    first_wrapped = 16 * WLAT - s
    window_row = jnp.where(late_row, (lat + 15) % 16, lat) * WLAT
    wk = jnp.where(window_row + ri >= first_wrapped, 1, 0)
    wqv = jnp.where(window_row + qri >= first_wrapped, 1, 0)
    kk = iota((TOK, GT), 0)
    fold[...] = jnp.where(kk == tq, 1.0, 0.0).astype(BF)
    fh = lax.shift_right_logical(iota((GW, GT), 0), 5)
    lane_t = iota((GW, GT), 1)
    hmask[...] = jnp.where((lane_t >= fh * TOK) & (lane_t < (fh + 1) * TOK), 1.0, 0.0).astype(BF)
    group_head = lax.shift_right_logical(iota((TOK, GW), 1), 5)
    eye = jnp.where(iota((GW, GW), 0) == iota((GW, GW), 1), 1.0, 0.0).astype(BF)
    scale_rows = [
        lanes_of([stemp_ref[g * GRP + h] * SCALE for h in range(GRP)], (1, GT), 1, TOK) for g in range(2)
    ]
    n = iota((256, 1), 0)
    bit = lambda shift, mask: lax.shift_right_logical(n, shift) & mask
    wrow = bit(7, 1) * 256 + bit(4, 3) * 64 + core * 32 + bit(1, 7) * 4 + bit(6, 1) * 2 + (n & 1)
    pick = one_hot(wrow, n >= 0, D)

    back_own, back_side, back_far, bedge_own, bedge_side = two_step_matrices(
        -row_step, -col_step, True, not late_col, own_place, window_index
    )
    pltpu.make_async_copy(wq_hbm, wq, wq_sem).wait()
    arrived(C_EE)
    beside = rl_e[THREE_DIAG - 8 : THREE_DIAG, :].astype(F32) if late_col else kvp[...]
    end = THREE_AT if late_col else SIDES
    valid_2 = jnp.where(late_row, rl_e[end - 8 : end, :].astype(F32), beside)
    lane = iota((TOK, 128), 1)
    valid_row = jnp.zeros((TOK, 128), F32)
    for r in range(WLAT):
        valid_row = jnp.where(ri == r, valid_2[r : r + 1, :128], valid_row)
    valid_k = jnp.sum(jnp.where(lane == cj, valid_row, 0.0), 1, keepdims=True)
    ok = (wk == wqv) & ((valid_k > 0.5) | (kk == tq))
    bias[...] = jnp.where(ok, 0.0, NEG)
    rolled = near + nn(sel_side, rl_e[...])

    mean = jnp.mean(rolled, 1, keepdims=True)
    centered = rolled - mean
    inv = lax.rsqrt(jnp.mean(centered * centered, 1, keepdims=True) + EPS)
    unit_v = centered * inv
    unit[...] = unit_v
    normed[...] = unit_v.astype(BF)
    send(normed, m_normed, C_TN, mate)
    qkv[...] = nn(normed[...], wq[...]).astype(BF)
    for g in range(2):
        lanes = slice(g * GW, (g + 1) * GW)
        qg = qkv[:, g * D : g * D + GW]
        for h in range(GRP):
            qs[g, h * TOK : (h + 1) * TOK, :] = jnp.where(group_head == h, qg, jnp.zeros_like(qg))
        st = nt(qkv[:, g * D + GW : (g + 1) * D], qs[g]) * scale_rows[g] + bias[...]
        e = jnp.exp(st - jnp.max(st, 0, keepdims=True))
        p = e * (1.0 / jnp.sum(e, 0, keepdims=True))
        pt[g] = p
        p16[g] = p.astype(BF)
        v_t = nt(eye, qkv[:, 2 * D + g * GW : 2 * D + (g + 1) * GW]).astype(BF)
        c_t = nn(v_t, p16[g]).astype(BF) * hmask[...]
        ctx[:, lanes] = nt(fold[...], c_t).astype(BF)
    send(ctx, m_ctx, C_TC, mate)
    load_wo.wait()
    att[...] = nn(ctx[...], wo[...]).astype(BF)
    pk_a[...] = nn(pack_back, att[...]).astype(BF)
    send(pk_a, rl_a, C_AW, lon_back)

    arrived(C_GN)
    rgrad[...] = (near_g + nn(two_far, rn_g[...])).astype(BF)
    send(rgrad, m_rgrad, C_TR, mate)
    cgrad = nt(rgrad[...], wo[...]).astype(BF)
    for g in range(2):
        piece = cgrad[:, g * GW : (g + 1) * GW]
        for h in range(GRP):
            cgs[g, h * TOK : (h + 1) * TOK, :] = jnp.where(group_head == h, piece, jnp.zeros_like(piece))
    for g in range(2):
        qgrad[:, 2 * D + g * GW : 2 * D + (g + 1) * GW] = nn(p16[g], cgs[g]).astype(BF)
    third = [pl.ds(k * D, D) for k in range(3)]
    send(qgrad.at[:, third[2]], m_qgrad.at[:, third[2]], C_TV, mate)

    def scores_back(g):
        p = pt[g]
        dp = nt(qkv[:, 2 * D + g * GW : 2 * D + (g + 1) * GW], cgs[g])
        ds = p * (dp - jnp.sum(p * dp, 0, keepdims=True)) * scale_rows[g]
        ds16 = ds.astype(BF)
        k_t = nt(eye, qkv[:, g * D + GW : (g + 1) * D]).astype(BF)
        q_t = nn(k_t, ds16).astype(BF) * hmask[...]
        qgrad[:, g * D : g * D + GW] = nt(fold[...], q_t).astype(BF)
        qgrad[:, g * D + GW : (g + 1) * D] = nn(ds16, qs[g]).astype(BF)
        send(qgrad.at[:, third[g]], m_qgrad.at[:, third[g]], C_TQ0 + g, mate)

    def picked(left, m_left):
        return nt(pick, left[...]).astype(BF), nt(pick, m_left[...]).astype(BF)

    def chip_sum(lefts, right, m_right):
        total = nn(lefts[0], right) + nn(lefts[1], m_right)
        return total.astype(BF).reshape(NY, NX, 16, right.shape[1])

    def share(low_a, width_a, low_b, width_b):
        a, b = pl.ds(low_a, width_a), pl.ds(low_b, width_b)
        for k in range(1, NY):
            send(send_a.at[(y + k) % NY, :, :, a], r1a.at[k - 1, :, :, a], C_1A, y_peers[k - 1], r1a)
        for k in range(1, NX):
            send(send_b.at[:, (x + k) % NX, :, b], r1b.at[k - 1, :, :, b], C_1B, x_peers[k - 1], r1b)

    arrived(C_TC)
    arrived(C_TR)
    g_out = chip_sum(picked(ctx, m_ctx), rgrad[...], m_rgrad[...])
    send_a[:, :, :, 768:] = g_out[:, :, :, :256]
    send_b[:, :, :, 768:] = g_out[:, :, :, 256:]
    share(768, 256, 768, 256)
    scores_back(0)
    arrived(C_TN)
    arrived(C_TV)
    lefts = picked(normed, m_normed)
    g_val = chip_sum(lefts, qgrad[:, 2 * D :], m_qgrad[:, 2 * D :])
    send_a[:, :, :, 384:768] = g_val[:, :, :, :384]
    send_b[:, :, :, 640:768] = g_val[:, :, :, 384:]
    share(384, 384, 640, 128)
    scores_back(1)

    def sum_qk(g):
        arrived(C_TQ0 + g)
        return chip_sum(lefts, qgrad[:, g * D : (g + 1) * D], m_qgrad[:, g * D : (g + 1) * D])

    g_qk = sum_qk(0)
    send_a[:, :, :, :256] = g_qk[:, :, :, :256]
    send_b[:, :, :, :256] = g_qk[:, :, :, 256:]
    share(0, 256, 0, 256)
    ugrad = nt(qgrad[...], wq[...])
    u = unit[...]
    xgrad = inv * (
        ugrad - jnp.mean(ugrad, 1, keepdims=True) - u * jnp.mean(ugrad * u, 1, keepdims=True)
    )
    xg[...] = xgrad.astype(BF)
    pk_x[...] = nn(pack_back, xg[...]).astype(BF)
    send(pk_x, rl_x, C_XW, lon_back)
    g_qk = sum_qk(1)
    send_a[:, :, :, 256:384] = g_qk[:, :, :, :128]
    send_b[:, :, :, 256:640] = g_qk[:, :, :, 128:]
    share(256, 128, 256, 384)
    near_x = own_g[...].astype(F32) + nn(back_own, xg[...])
    key_q = nt(q_rows, kvw[:, :D]).astype(BF)
    edge_x = nn(bedge_own, xg[...])
    arrived(C_AW)
    sn_a[...] = (nn(bedge_own, att[...]) + nn(bedge_side, rl_a[...])).astype(BF)
    near_a = nn(back_own, att[...]) + nn(back_side, rl_a[...])
    arrived(C_XW)
    sn_x[...] = (edge_x + nn(bedge_side, rl_x[...])).astype(BF)
    send_lat(sn_x, rn_x, C_XS, north, south)
    near_x = near_x + nn(back_side, rl_x[...])
    arrived(C_1A)
    arrived(C_1B)
    sum_a = send_a[y].astype(F32)
    sum_b = send_b[:, x].astype(F32)
    for k in range(3):
        sum_a = sum_a + r1a[k].astype(F32)
        sum_b = sum_b + r1b[k].astype(F32)
    s2a[...] = sum_a.astype(BF)
    s2b[...] = sum_b.astype(BF)
    for k in range(1, NX):
        send(s2a.at[(x + k) % NX], r2a.at[k - 1], C_2A, x_peers[k - 1], r2a)
    for k in range(1, NY):
        send(s2b.at[(y + k) % NY], r2b.at[k - 1], C_2B, y_peers[k - 1], r2b)
    arrived(C_XS)
    send_lat(sn_a, rn_a, C_AS, north, south)
    egrad = (near_x + nn(back_far, rn_x[...])).astype(BF)

    cback[...] = nt(egrad, eo[...]).astype(BF).astype(F32)

    for p in range(HALF):
        rows = slice(p * PADL, (p + 1) * PADL)
        c0 = cback[p : p + 1, :]
        c1 = cback[HALF + p : HALF + p + 1, :]
        v = vals[rows, :].astype(F32)
        prod[rows, :D] = (c0 * v).astype(BF)
        prod[rows, D:] = (c1 * v).astype(BF)
        vgrad[rows, :] = (wexp[rows, :D].astype(F32) * c0 + wexp[rows, D:].astype(F32) * c1).astype(BF)

    for c in range(ROWS // CHUNK):
        rows = slice(c * CHUNK, (c + 1) * CHUNK)
        pg = nt(prod[rows, :], spread).reshape(CHUNK // PADL, PADL, 2 * HEADS)
        pm = prob[rows, :].reshape(CHUNK // PADL, PADL, 2 * HEADS)
        sg = pm * (pg - jnp.sum(pm * pg, 1, keepdims=True))
        prob[rows, :] = sg.reshape(CHUNK, 2 * HEADS) * lane_scale

    def level_grads(c):
        rows = slice(c * CHUNK, (c + 1) * CHUNK)
        lg = nt(vgrad[rows, :], kvw[:, D:]) + nn(prob[rows, :].astype(BF), key_q)
        lg = lg.astype(BF).reshape(CHUNK // PADL, PADL, D)
        for k in range(4):
            lg_v[run_of(4 * c + k) : run_of(4 * c + k) + 6] = lg[6 * k : 6 * (k + 1), :LEVELS, :]

    arrived(C_2A)
    arrived(C_2B)
    last_a = s2a[x].astype(F32)
    last_b = s2b[y].astype(F32)
    for k in range(3):
        last_a = last_a + r2a[k].astype(F32)
        last_b = last_b + r2b[k].astype(F32)
    for j in range(8):
        value = (last_a if j < 4 else last_b)[:, 256 * (j % 4) : 256 * (j % 4 + 1)]
        for h in range(2):
            s3f[h, pl.ds(j, 16, stride=8), :] = value[:, 128 * h : 128 * (h + 1)]
    for k in range(NZ):
        for h in range(2):
            s3[k, :, 128 * h : 128 * (h + 1)] = s3f[h, 16 * k : 16 * (k + 1), :].astype(BF)
    for k in range(1, NZ):
        send(s3.at[(z + k) % NZ], r3.at[k - 1], C_3, z_peers[k - 1], r3)

    for c in range(3):
        level_grads(c)
    stores = [pltpu.make_async_copy(lg_v, lg_hbm, lsem.at[len(loads) + 1])]
    stores[-1].start()
    arrived(C_AS)
    added = near_a + nn(back_far, rn_a[...])
    out16 = (own_e[...].astype(F32) + added).astype(BF)
    u_row = iota((TOK, 1), 0)
    u_patch = lax.shift_right_logical(u_row, 1)
    u_lat = lax.shift_right_logical(u_patch * 171, 11)
    together = one_hot(own_index(u_row & 1, u_lat, u_patch - u_lat * WLON), u_row >= 0, TOK)
    rows_f[...] = nn(together, out16)
    for p in range(HALF):
        out_v[p] = rows_f[2 * p : 2 * p + 2, :].astype(BF)
    stores.append(pltpu.make_async_copy(out_v, out_hbm, lsem.at[len(loads) + 2]))
    stores[-1].start()

    arrived(C_3)
    factor = GRAD_GAIN * (2 * 96 * 192) ** (-0.5)
    for h in range(2):
        total = s3f[h, pl.ds(pl.multiple_of(16 * z, 16), 16), :]
        for k in range(NZ - 1):
            total = total + r3[k, :, 128 * h : 128 * (h + 1)].astype(F32)
        total = total * factor
        for b in range(2):
            for j in range(8):
                piece = total[8 * b + j : 8 * b + j + 1, :]
                place = PIECES[j // 4][2 * (j % 4) + h]
                if place < 12:
                    gq_ref[12 * b + place : 12 * b + place + 1, :] = piece
                else:
                    go_ref[4 * b + place - 12 : 4 * b + place - 11, :] = piece
    for i, (src, dst) in enumerate(((gq_ref, gq_hbm), (go_ref, go_hbm))):
        stores.append(pltpu.make_async_copy(src, dst, lsem.at[len(loads) + 3 + i]))
        stores[-1].start()
    for index in landings:
        whole(index).wait_send()
    for copy in stores:
        copy.wait()


def deliver(a, b, c, d, a_out, b_out, c_out, d_out, sems):
    pairs = ((a, a_out), (b, b_out), (c, c_out), (d, d_out))
    copies = [pltpu.make_async_copy(src, dst, sems.at[i]) for i, (src, dst) in enumerate(pairs)]
    for copy in copies:
        copy.start()
    for copy in copies:
        copy.wait()


def local(levels_in, latent_queries, enc_kv, enc_out, enc_temp, w_qkv, w_out, swin_temp, lat_shift, lon_shift, key_valid, output_grad):
    hbm = pl.BlockSpec(memory_space=pl.ANY)
    V = pltpu.VMEM
    block = lambda rows: V((rows, D), BF)
    scratch = [
        V((HALF, LEVELS, D), BF), V((D, 2 * D), BF), V((D, D), BF), V((D, 3 * D), BF), V((D, D), BF), V((HALF, 2, D), BF),
        V((2, D), BF), pltpu.SMEM((HEADS,), F32), pltpu.SMEM((HEADS,), F32), pltpu.SMEM((1,), jnp.int32),
        pltpu.SMEM((1,), jnp.int32), V((WLAT, WLON), jnp.int32),
        V((ROWS, D), BF),
        V((ROWS, D), BF),
        V((ROWS, 2 * HEADS), F32),
        V((ROWS, 2 * D), BF),
        V((ROWS, 2 * D), BF),
        V((ROWS, D), BF),
        V((8, 8 * HALF, 128), F32),
        V((TOK, D), F32),
        V((TOK, D), F32),
        V((8, D), F32),
        V((HALF, 2, D), BF),
        V((HALF, LEVELS, D), BF),
        V((24, 128), F32), V((8, 128), F32),
    ]
    scratch += [block(TOK), block(SIDES), block(SIDES)]
    for _ in range(3):
        scratch += [block(TOK), block(THREE), block(THREE), block(BOTH), block(BOTH)]
    scratch += [
        V((TOK, D), F32), V((TOK, 3 * D), BF), block(TOK), block(TOK), block(TOK), V((TOK, 3 * D), BF),
        block(TOK), block(TOK), block(TOK), V((TOK, 3 * D), BF),
        V((2, GT, GW), BF), V((2, GT, GW), BF), V((2, TOK, GT), F32), V((2, TOK, GT), BF),
        V((TOK, GT), F32), V((GW, GT), BF), V((TOK, GT), BF),
        V((NY, NX, 16, WIDE), BF), V((NY, NX, 16, WIDE), BF),
        V((3, NX, 16, WIDE), BF), V((3, NY, 16, WIDE), BF),
        V((NX, 16, WIDE), BF), V((NY, 16, WIDE), BF),
        V((3, 16, WIDE), BF), V((3, 16, WIDE), BF),
        V((2, 128, 128), F32), V((NZ, 16, 256), BF), V((NZ - 1, 16, 256), BF),
        pltpu.SemaphoreType.DMA((16,)),
        pltpu.SemaphoreType.DMA((N_COPY,)),
        pltpu.SemaphoreType.DMA((N_COPY,)),
    ]
    lev = jnp.transpose(levels_in, (1, 2, 0, 3)).reshape(HALF, LEVELS, D)
    og = jnp.transpose(output_grad, (1, 2, 0, 3)).reshape(HALF, 2, D)
    shapes = (
        jax.ShapeDtypeStruct((HALF, 2, D), BF),
        jax.ShapeDtypeStruct((HALF, LEVELS, D), BF),
        jax.ShapeDtypeStruct((24, 128), F32),
        jax.ShapeDtypeStruct((8, 128), F32),
    )

    def run(late_col):
        return pl.pallas_call(
            functools.partial(kernel, late_col),
            out_shape=shapes,
            in_specs=[hbm] * 12,
            out_specs=(hbm,) * 4,
            scratch_shapes=scratch,
            compiler_params=pltpu.CompilerParams(
                collective_id=int(late_col), has_side_effects=True, vmem_limit_bytes=48 * 1024 * 1024
            ),
        )

    parts = lax.cond(
        lon_shift[0] > WLON // 2, run(True), run(False),
        lev, latent_queries, enc_kv, enc_out, enc_temp, w_qkv, w_out, swin_temp, lat_shift, lon_shift, key_valid, og,
    )
    out, lg, gq, go = pl.pallas_call(
        deliver,
        out_shape=shapes,
        in_specs=[hbm] * 4,
        out_specs=(hbm,) * 4,
        scratch_shapes=[pltpu.SemaphoreType.DMA((4,))],
    )(*parts)
    out = jnp.transpose(out.reshape(WLAT, WLON, 2, D), (2, 0, 1, 3))
    lg = jnp.transpose(lg.reshape(WLAT, WLON, LEVELS, D), (2, 0, 1, 3))
    return out, lg, gq.reshape(-1), go.reshape(-1)


def solution(mesh):
    return jax.shard_map(
        local,
        mesh=mesh,
        in_specs=(
            P(None, "lat", "lon", None), P(), P(), P(), P(), P(), P(), P(), P(), P(),
            P("lat", "lon"),
            P(None, "lat", "lon", None),
        ),
        out_specs=(
            P(None, "lat", "lon", None),
            P(None, "lat", "lon", None),
            P(("lat", "lon")),
            P(("lat", "lon")),
        ),
        check_vma=False,
    )
```

time: 52.4 us -> 47.9 us (0.914)
  the two profiles are of different devices: /device:TPU:16 before, /device:TPU:1 now
where the time goes in v3:
time: 47.9 us; the launch traced here: 47.8 us
  Pallas kernels  46.1 us (96%)
  between operations  1.45 us (3%)
    pallas_call x1, Pallas kernels, local(): lax.cond(lon_shift[0] > WLON // 2, run(True), run(False), lev, latent_que...  45 us
    pallas_call x1, Pallas kernels, local(): pl.pallas_call(deliver, out_shape=shapes, in_specs=[hbm] * 4, out_specs=(...  1.1 us

profile of v3, /device:TPU:1, one launch (start us, length us, event | category | flops | bytes accessed | tf_op | source)
XLA Modules:
  0.0 47.8 jit_solution(2758040783301393202)
XLA Ops:
  1.3 45.2 %conditional.1 = ((bf16[72,2,512]{2,1,0:T(2,128)(2,1)S(1)}, bf16[72,13,512]{2,1,0:T(8,128)(2,1)S(1)}, f32[24,128]{1,0:T(8,128)S(1)}, f32[8,128]{1,0:T(8,128)S(1)})) conditional(s32[]{:T(128)} %bitcast, (bf16[72,13,512]{2,1,0:T(8,128)(2,1)}, bf16[2,512]{1,0:T(2,128)(2,1)}, bf16[512,1024]{1,0:T(8,128)(2,1)}, bf16[512,512]{1,0:T(8,128)(2,1)}, ...), branch_computations={%region_0.0_spmd, %region_1.0_spmd} | conditional | bytes 8 | solution.py:692
  1.5 45.0 %branch_1_fun.1 = (bf16[72,2,512]{2,1,0:T(2,128)(2,1)S(1)}, bf16[72,13,512]{2,1,0:T(8,128)(2,1)S(1)}, f32[24,128]{1,0:T(8,128)S(1)}, f32[8,128]{1,0:T(8,128)S(1)}) custom-call(bf16[72,13,512]{2,1,0:T(8,128)(2,1)} %get-tuple-element.60.lev_hbm, bf16[2,512]{1,0:T(2,128)(2,1)} %get-tuple-element.61.q_hbm, bf16[512,1024]{1,0:T(8,128)(2,1)} %get-tuple-element.62.kvw_hbm, ...), custom_call_target="tpu_custom_call" | custom-call | tf_op jit(solution)/shard_map/cond/branch_1_fun/pallas_call | solution.py:692
  46.5 1.1 %shard_map.147 = (bf16[72,2,512]{2,1,0:T(2,128)(2,1)}, bf16[72,13,512]{2,1,0:T(8,128)(2,1)}, f32[24,128]{1,0:T(8,128)}, f32[8,128]{1,0:T(8,128)}) custom-call(bf16[72,2,512]{2,1,0:T(2,128)(2,1)S(1)} %get-tuple-element.84.a, bf16[72,13,512]{2,1,0:T(8,128)(2,1)S(1)} %get-tuple-element.85.b, f32[24,128]{1,0:T(8,128)S(1)} %get-tuple-element.86.c, ...), custom_call_target="tpu_custom_call" | custom-call | tf_op jit(solution)/shard_map/pallas_call | solution.py:696

commit v4 on v3

--- a/solution.py
+++ b/solution.py
@@ -32,8 +32,9 @@
 SCALE = 1.0 / math.sqrt(HD)
 
 NY, NX, NZ = 4, 4, 8
-WIDE = 1024
-PIECES = ((0, 1, 2, 8, 9, 10, 12, 13), (4, 5, 3, 6, 7, 11, 14, 15))
+WIDTHS = ((512, 512), (384, 640))
+PIECES = (0, 1, 2, 4, 5, 3, 6, 7, 8, 9, 12, 13, 10, 11, 14, 15)
+
 EDGES = (0, 80, 128, 160, 240, 304)
 PLACES = tuple(zip(EDGES[:-1], EDGES[1:]))
 LON_AT, THREE_DIAG, TWO_DIAG, THREE_AT, TWO_AT, SIDES = EDGES
@@ -41,9 +42,9 @@
 FIRST = 40
 
 (
-    C_EE, C_GE, C_AW, C_XW, C_TN, C_TR, C_TC, C_TV, C_TQ0, C_TQ1, C_GN, C_AS, C_XS, C_1A, C_1B, C_2A, C_2B, C_3,
-) = range(18)
-N_COPY = 18
+    C_EE, C_GE, C_AW, C_XW, C_TN, C_TR, C_TC, C_TV, C_TQ0, C_TQ1, C_GN, C_AS, C_XS, C_1, C_1B, C_1LA, C_1LB, C_2, C_2B, C_2LA, C_2LB, C_3,
+) = range(22)
+N_COPY = 22
 THREE, BOTH = 80, 144
 
 
@@ -176,7 +177,7 @@
     unit, qkv, normed, rgrad, ctx, qgrad,
     m_normed, m_rgrad, m_ctx, m_qgrad,
     qs, cgs, pt, p16, bias, hmask, fold,
-    send_a, send_b, r1a, r1b, s2a, s2b, r2a, r2b, s3f, s3, r3,
+    early, late, s3f, s3, r3,
     lsem, ssem, rsem,
 ):
     lat = lax.axis_index("lat")
@@ -202,10 +203,6 @@
     lon_ahead, lon_back = (east, west) if late_col else (west, east)
     ahead = (lon_ahead, (south[0], lon_ahead[1]), (north[0], lon_ahead[1]), south, north)
     greeted = [mate, *ahead, lon_back, (north[0], lon_back[1]), (south[0], lon_back[1])] + y_peers + x_peers + z_peers
-    barrier = pltpu.get_barrier_semaphore()
-    for peer in greeted:
-        pl.semaphore_signal(barrier, inc=1, device_id=peer, device_id_type=MESH)
-
     loads = []
 
     def load(src, dst):
@@ -213,6 +210,12 @@
         loads[-1].start()
         return loads[-1]
 
+    load_og = load(og_hbm, og)
+    load_kvw = load(kvw_hbm, kvw)
+    load_lev = load(lev_hbm, lev)
+    barrier = pltpu.get_barrier_semaphore()
+    for peer in greeted:
+        pl.semaphore_signal(barrier, inc=1, device_id=peer, device_id_type=MESH)
     small = [
         load(src, dst)
         for src, dst in (
@@ -220,9 +223,7 @@
             (etemp_hbm, etemp_ref), (stemp_hbm, stemp_ref),
         )
     ]
-    load_og = load(og_hbm, og)
-    load_kvw = load(kvw_hbm, kvw)
-    load_lev = load(lev_hbm, lev)
+
     landings = {}
 
     def send(src, dst, index, peer, landing=None):
@@ -365,10 +366,6 @@
     )
     near_g = nn(two_own, own_g[...])
     edge_g = nn(two_edge_own, own_g[...])
-    arrived(C_GE)
-    sn_g[...] = (edge_g + nn(two_edge_side, rl_g[...])).astype(BF)
-    send_lat(sn_g, rn_g, C_GN, south, north)
-    near_g = near_g + nn(two_side, rl_g[...])
     tq = iota((1, GT), 1)
     for k in range(1, GRP):
         tq = jnp.where(iota((1, GT), 1) >= k * TOK, iota((1, GT), 1) - k * TOK, tq)
@@ -396,6 +393,10 @@
         -row_step, -col_step, True, not late_col, own_place, window_index
     )
     pltpu.make_async_copy(wq_hbm, wq, wq_sem).wait()
+    arrived(C_GE)
+    sn_g[...] = (edge_g + nn(two_edge_side, rl_g[...])).astype(BF)
+    send_lat(sn_g, rn_g, C_GN, south, north)
+    near_g = near_g + nn(two_side, rl_g[...])
     arrived(C_EE)
     beside = rl_e[THREE_DIAG - 8 : THREE_DIAG, :].astype(F32) if late_col else kvp[...]
     end = THREE_AT if late_col else SIDES
@@ -417,25 +418,28 @@
     normed[...] = unit_v.astype(BF)
     send(normed, m_normed, C_TN, mate)
     qkv[...] = nn(normed[...], wq[...]).astype(BF)
+    scores, values_t, turned = [], [], []
     for g in range(2):
-        lanes = slice(g * GW, (g + 1) * GW)
         qg = qkv[:, g * D : g * D + GW]
         for h in range(GRP):
             qs[g, h * TOK : (h + 1) * TOK, :] = jnp.where(group_head == h, qg, jnp.zeros_like(qg))
-        st = nt(qkv[:, g * D + GW : (g + 1) * D], qs[g]) * scale_rows[g] + bias[...]
+        scores.append(nt(qkv[:, g * D + GW : (g + 1) * D], qs[g]))
+    for g in range(2):
+        values_t.append(nt(eye, qkv[:, 2 * D + g * GW : 2 * D + (g + 1) * GW]).astype(BF))
+    for g in range(2):
+        st = scores[g] * scale_rows[g] + bias[...]
         e = jnp.exp(st - jnp.max(st, 0, keepdims=True))
         p = e * (1.0 / jnp.sum(e, 0, keepdims=True))
         pt[g] = p
         p16[g] = p.astype(BF)
-        v_t = nt(eye, qkv[:, 2 * D + g * GW : 2 * D + (g + 1) * GW]).astype(BF)
-        c_t = nn(v_t, p16[g]).astype(BF) * hmask[...]
-        ctx[:, lanes] = nt(fold[...], c_t).astype(BF)
+        turned.append(nn(values_t[g], p16[g]).astype(BF) * hmask[...])
+    for g in range(2):
+        ctx[:, g * GW : (g + 1) * GW] = nt(fold[...], turned[g]).astype(BF)
     send(ctx, m_ctx, C_TC, mate)
     load_wo.wait()
     att[...] = nn(ctx[...], wo[...]).astype(BF)
     pk_a[...] = nn(pack_back, att[...]).astype(BF)
     send(pk_a, rl_a, C_AW, lon_back)
-
     arrived(C_GN)
     rgrad[...] = (near_g + nn(two_far, rn_g[...])).astype(BF)
     send(rgrad, m_rgrad, C_TR, mate)
@@ -467,27 +471,57 @@
         total = nn(lefts[0], right) + nn(lefts[1], m_right)
         return total.astype(BF).reshape(NY, NX, 16, right.shape[1])
 
-    def share(low_a, width_a, low_b, width_b):
+    def share(k_set, low_a, width_a, low_b, width_b):
+        send_a, send_b, r1a, r1b = (early, late)[k_set][:4]
         a, b = pl.ds(low_a, width_a), pl.ds(low_b, width_b)
         for k in range(1, NY):
-            send(send_a.at[(y + k) % NY, :, :, a], r1a.at[k - 1, :, :, a], C_1A, y_peers[k - 1], r1a)
+            src = send_a.at[(y + k) % NY, :, :, a]
+            send(src, r1a.at[k - 1, :, :, a], C_1 + 2 * k_set, y_peers[k - 1], r1a)
         for k in range(1, NX):
-            send(send_b.at[:, (x + k) % NX, :, b], r1b.at[k - 1, :, :, b], C_1B, x_peers[k - 1], r1b)
-
+            src = send_b.at[:, (x + k) % NX, :, b]
+            send(src, r1b.at[k - 1, :, :, b], C_1 + 2 * k_set + 1, x_peers[k - 1], r1b)
+
+    def second_stage(k_set):
+        send_a, send_b, r1a, r1b, s2a, s2b, r2a, r2b = (early, late)[k_set]
+        arrived(C_1 + 2 * k_set)
+        arrived(C_1 + 2 * k_set + 1)
+        sum_a = send_a[y].astype(F32)
+        sum_b = send_b[:, x].astype(F32)
+        for k in range(3):
+            sum_a = sum_a + r1a[k].astype(F32)
+            sum_b = sum_b + r1b[k].astype(F32)
+        s2a[...] = sum_a.astype(BF)
+        s2b[...] = sum_b.astype(BF)
+        for k in range(1, NX):
+            send(s2a.at[(x + k) % NX], r2a.at[k - 1], C_2 + 2 * k_set, x_peers[k - 1], r2a)
+        for k in range(1, NY):
+            send(s2b.at[(y + k) % NY], r2b.at[k - 1], C_2 + 2 * k_set + 1, y_peers[k - 1], r2b)
+
+    def second_sums(k_set):
+        s2a, s2b, r2a, r2b = (early, late)[k_set][4:]
+        arrived(C_2 + 2 * k_set)
+        arrived(C_2 + 2 * k_set + 1)
+        sum_a = s2a[x].astype(F32)
+        sum_b = s2b[y].astype(F32)
+        for k in range(3):
+            sum_a = sum_a + r2a[k].astype(F32)
+            sum_b = sum_b + r2b[k].astype(F32)
+        return sum_a, sum_b
+
+    scores_back(0)
     arrived(C_TC)
     arrived(C_TR)
     g_out = chip_sum(picked(ctx, m_ctx), rgrad[...], m_rgrad[...])
-    send_a[:, :, :, 768:] = g_out[:, :, :, :256]
-    send_b[:, :, :, 768:] = g_out[:, :, :, 256:]
-    share(768, 256, 768, 256)
-    scores_back(0)
+    early[0][:, :, :, 256:] = g_out[:, :, :, :256]
+    early[1][:, :, :, 256:] = g_out[:, :, :, 256:]
+    share(0, 256, 256, 256, 256)
     arrived(C_TN)
     arrived(C_TV)
     lefts = picked(normed, m_normed)
     g_val = chip_sum(lefts, qgrad[:, 2 * D :], m_qgrad[:, 2 * D :])
-    send_a[:, :, :, 384:768] = g_val[:, :, :, :384]
-    send_b[:, :, :, 640:768] = g_val[:, :, :, 384:]
-    share(384, 384, 640, 128)
+    early[0][:, :, :, :256] = g_val[:, :, :, :256]
+    early[1][:, :, :, :256] = g_val[:, :, :, 256:]
+    share(0, 0, 256, 0, 256)
     scores_back(1)
 
     def sum_qk(g):
@@ -495,9 +529,9 @@
         return chip_sum(lefts, qgrad[:, g * D : (g + 1) * D], m_qgrad[:, g * D : (g + 1) * D])
 
     g_qk = sum_qk(0)
-    send_a[:, :, :, :256] = g_qk[:, :, :, :256]
-    send_b[:, :, :, :256] = g_qk[:, :, :, 256:]
-    share(0, 256, 0, 256)
+    late[0][:, :, :, :256] = g_qk[:, :, :, :256]
+    late[1][:, :, :, :256] = g_qk[:, :, :, 256:]
+    share(1, 0, 256, 0, 256)
     ugrad = nt(qgrad[...], wq[...])
     u = unit[...]
     xgrad = inv * (
@@ -507,46 +541,49 @@
     pk_x[...] = nn(pack_back, xg[...]).astype(BF)
     send(pk_x, rl_x, C_XW, lon_back)
     g_qk = sum_qk(1)
-    send_a[:, :, :, 256:384] = g_qk[:, :, :, :128]
-    send_b[:, :, :, 256:640] = g_qk[:, :, :, 128:]
-    share(256, 128, 256, 384)
+    late[0][:, :, :, 256:] = g_qk[:, :, :, :128]
+    late[1][:, :, :, 256:] = g_qk[:, :, :, 128:]
+    share(1, 256, 128, 256, 384)
     near_x = own_g[...].astype(F32) + nn(back_own, xg[...])
     key_q = nt(q_rows, kvw[:, :D]).astype(BF)
     edge_x = nn(bedge_own, xg[...])
-    arrived(C_AW)
-    sn_a[...] = (nn(bedge_own, att[...]) + nn(bedge_side, rl_a[...])).astype(BF)
-    near_a = nn(back_own, att[...]) + nn(back_side, rl_a[...])
+    second_stage(0)
     arrived(C_XW)
     sn_x[...] = (edge_x + nn(bedge_side, rl_x[...])).astype(BF)
     send_lat(sn_x, rn_x, C_XS, north, south)
     near_x = near_x + nn(back_side, rl_x[...])
-    arrived(C_1A)
-    arrived(C_1B)
-    sum_a = send_a[y].astype(F32)
-    sum_b = send_b[:, x].astype(F32)
-    for k in range(3):
-        sum_a = sum_a + r1a[k].astype(F32)
-        sum_b = sum_b + r1b[k].astype(F32)
-    s2a[...] = sum_a.astype(BF)
-    s2b[...] = sum_b.astype(BF)
-    for k in range(1, NX):
-        send(s2a.at[(x + k) % NX], r2a.at[k - 1], C_2A, x_peers[k - 1], r2a)
-    for k in range(1, NY):
-        send(s2b.at[(y + k) % NY], r2b.at[k - 1], C_2B, y_peers[k - 1], r2b)
+    second_stage(1)
     arrived(C_XS)
+    arrived(C_AW)
+    sn_a[...] = (nn(bedge_own, att[...]) + nn(bedge_side, rl_a[...])).astype(BF)
     send_lat(sn_a, rn_a, C_AS, north, south)
     egrad = (near_x + nn(back_far, rn_x[...])).astype(BF)
 
     cback[...] = nt(egrad, eo[...]).astype(BF).astype(F32)
 
-    for p in range(HALF):
-        rows = slice(p * PADL, (p + 1) * PADL)
-        c0 = cback[p : p + 1, :]
-        c1 = cback[HALF + p : HALF + p + 1, :]
-        v = vals[rows, :].astype(F32)
-        prod[rows, :D] = (c0 * v).astype(BF)
-        prod[rows, D:] = (c1 * v).astype(BF)
-        vgrad[rows, :] = (wexp[rows, :D].astype(F32) * c0 + wexp[rows, D:].astype(F32) * c1).astype(BF)
+    def products(c, carry):
+        first = cback[pl.ds(pl.multiple_of(8 * c, 8), 8), :]
+        second = cback[pl.ds(pl.multiple_of(HALF + 8 * c, 8), 8), :]
+        for p in range(8):
+            rows = pl.ds(pl.multiple_of(8 * PADL * c + p * PADL, PADL), PADL)
+            c0, c1 = first[p : p + 1, :], second[p : p + 1, :]
+            v = vals[rows, :].astype(F32)
+            prod[rows, :D] = (c0 * v).astype(BF)
+            prod[rows, D:] = (c1 * v).astype(BF)
+            vgrad[rows, :] = (wexp[rows, :D].astype(F32) * c0 + wexp[rows, D:].astype(F32) * c1).astype(BF)
+        return carry
+
+    lax.fori_loop(0, HALF // 8, products, 0)
+
+    sums = [*second_sums(1), *second_sums(0)]
+    chunks = [v[:, 128 * i : 128 * (i + 1)] for v in sums for i in range(v.shape[1] // 128)]
+    for i, value in enumerate(chunks):
+        s3f[i % 2, pl.ds(i // 2, 16, stride=8), :] = value
+    for k in range(NZ):
+        for h in range(2):
+            s3[k, :, 128 * h : 128 * (h + 1)] = s3f[h, 16 * k : 16 * (k + 1), :].astype(BF)
+    for k in range(1, NZ):
+        send(s3.at[(z + k) % NZ], r3.at[k - 1], C_3, z_peers[k - 1], r3)
 
     for c in range(ROWS // CHUNK):
         rows = slice(c * CHUNK, (c + 1) * CHUNK)
@@ -562,29 +599,12 @@
         for k in range(4):
             lg_v[run_of(4 * c + k) : run_of(4 * c + k) + 6] = lg[6 * k : 6 * (k + 1), :LEVELS, :]
 
-    arrived(C_2A)
-    arrived(C_2B)
-    last_a = s2a[x].astype(F32)
-    last_b = s2b[y].astype(F32)
-    for k in range(3):
-        last_a = last_a + r2a[k].astype(F32)
-        last_b = last_b + r2b[k].astype(F32)
-    for j in range(8):
-        value = (last_a if j < 4 else last_b)[:, 256 * (j % 4) : 256 * (j % 4 + 1)]
-        for h in range(2):
-            s3f[h, pl.ds(j, 16, stride=8), :] = value[:, 128 * h : 128 * (h + 1)]
-    for k in range(NZ):
-        for h in range(2):
-            s3[k, :, 128 * h : 128 * (h + 1)] = s3f[h, 16 * k : 16 * (k + 1), :].astype(BF)
-    for k in range(1, NZ):
-        send(s3.at[(z + k) % NZ], r3.at[k - 1], C_3, z_peers[k - 1], r3)
-
     for c in range(3):
         level_grads(c)
     stores = [pltpu.make_async_copy(lg_v, lg_hbm, lsem.at[len(loads) + 1])]
     stores[-1].start()
     arrived(C_AS)
-    added = near_a + nn(back_far, rn_a[...])
+    added = nn(back_own, att[...]) + nn(back_side, rl_a[...]) + nn(back_far, rn_a[...])
     out16 = (own_e[...].astype(F32) + added).astype(BF)
     u_row = iota((TOK, 1), 0)
     u_patch = lax.shift_right_logical(u_row, 1)
@@ -606,7 +626,7 @@
         for b in range(2):
             for j in range(8):
                 piece = total[8 * b + j : 8 * b + j + 1, :]
-                place = PIECES[j // 4][2 * (j % 4) + h]
+                place = PIECES[2 * j + h]
                 if place < 12:
                     gq_ref[12 * b + place : 12 * b + place + 1, :] = piece
                 else:
@@ -659,10 +679,10 @@
         block(TOK), block(TOK), block(TOK), V((TOK, 3 * D), BF),
         V((2, GT, GW), BF), V((2, GT, GW), BF), V((2, TOK, GT), F32), V((2, TOK, GT), BF),
         V((TOK, GT), F32), V((GW, GT), BF), V((TOK, GT), BF),
-        V((NY, NX, 16, WIDE), BF), V((NY, NX, 16, WIDE), BF),
-        V((3, NX, 16, WIDE), BF), V((3, NY, 16, WIDE), BF),
-        V((NX, 16, WIDE), BF), V((NY, 16, WIDE), BF),
-        V((3, 16, WIDE), BF), V((3, 16, WIDE), BF),
+        *(
+            tuple(V((*lead, 16, w), BF) for lead in ((NY, NX), (3, NX), (NX,), (3,)) for w in pair)
+            for pair in WIDTHS
+        ),
         V((2, 128, 128), F32), V((NZ, 16, 256), BF), V((NZ - 1, 16, 256), BF),
         pltpu.SemaphoreType.DMA((16,)),
         pltpu.SemaphoreType.DMA((N_COPY,)),

time: 47.9 us -> 46.8 us (0.977)
  the two profiles are of different devices: /device:TPU:1 before, /device:TPU:16 now
where the time goes in v4:
time: 46.8 us; the launch traced here: 46.7 us
  Pallas kernels  45.1 us (96%)
  between operations  1.45 us (3%)
    pallas_call x1, Pallas kernels, local(): lax.cond(lon_shift[0] > WLON // 2, run(True), run(False), lev, latent_que...  43.9 us
    pallas_call x1, Pallas kernels, local(): pl.pallas_call(deliver, out_shape=shapes, in_specs=[hbm] * 4, out_specs=(...  1.1 us

profile of v4, /device:TPU:16, one launch (start us, length us, event | category | flops | bytes accessed | tf_op | source)
XLA Modules:
  0.0 46.7 jit_solution(10773054002961392007)
XLA Ops:
  1.3 44.1 %conditional.1 = ((bf16[72,2,512]{2,1,0:T(2,128)(2,1)S(1)}, bf16[72,13,512]{2,1,0:T(8,128)(2,1)S(1)}, f32[24,128]{1,0:T(8,128)S(1)}, f32[8,128]{1,0:T(8,128)S(1)})) conditional(s32[]{:T(128)} %bitcast, (bf16[72,13,512]{2,1,0:T(8,128)(2,1)}, bf16[2,512]{1,0:T(2,128)(2,1)}, bf16[512,1024]{1,0:T(8,128)(2,1)}, bf16[512,512]{1,0:T(8,128)(2,1)}, ...), branch_computations={%region_0.0_spmd, %region_1.0_spmd} | conditional | bytes 8 | solution.py:712
  1.3 43.9 %branch_0_fun.1 = (bf16[72,2,512]{2,1,0:T(2,128)(2,1)S(1)}, bf16[72,13,512]{2,1,0:T(8,128)(2,1)S(1)}, f32[24,128]{1,0:T(8,128)S(1)}, f32[8,128]{1,0:T(8,128)S(1)}) custom-call(bf16[72,13,512]{2,1,0:T(8,128)(2,1)} %get-tuple-element.48.lev_hbm, bf16[2,512]{1,0:T(2,128)(2,1)} %get-tuple-element.49.q_hbm, bf16[512,1024]{1,0:T(8,128)(2,1)} %get-tuple-element.50.kvw_hbm, ...), custom_call_target="tpu_custom_call" | custom-call | tf_op jit(solution)/shard_map/cond/branch_0_fun/pallas_call | solution.py:712
  45.4 1.1 %shard_map.147 = (bf16[72,2,512]{2,1,0:T(2,128)(2,1)}, bf16[72,13,512]{2,1,0:T(8,128)(2,1)}, f32[24,128]{1,0:T(8,128)}, f32[8,128]{1,0:T(8,128)}) custom-call(bf16[72,2,512]{2,1,0:T(2,128)(2,1)S(1)} %get-tuple-element.84.a, bf16[72,13,512]{2,1,0:T(8,128)(2,1)S(1)} %get-tuple-element.85.b, f32[24,128]{1,0:T(8,128)S(1)} %get-tuple-element.86.c, ...), custom_call_target="tpu_custom_call" | custom-call | tf_op jit(solution)/shard_map/pallas_call | solution.py:716

commit v5 on v4

--- a/solution.py
+++ b/solution.py
@@ -274,7 +274,6 @@
     late_row = s > WLAT // 2
     row_step = jnp.where(late_row, s - WLAT, s)
     col_step = t - WLON if late_col else t
-    sel_own, sel_side = roll_matrices(row_step, col_step, late_col)
     kvp[...] = jnp.zeros((8, D), F32)
     kvp[0:WLAT, 0:WLON] = valid_ref[...].astype(F32)
 
@@ -360,6 +359,7 @@
     own_e[...] = rows_f[...].astype(BF)
     pk_e[SIDES_1:, :] = with_valid(nn(pack_rest, own_e[...]), PLACES[3:])
     send_sides(PLACES[3:], ahead[3:])
+    sel_own, sel_side = roll_matrices(row_step, col_step, late_col)
     near = nn(sel_own, own_e[...])
     two_own, two_side, two_far, two_edge_own, two_edge_side = two_step_matrices(
         row_step, col_step, False, late_col, split_token, own_index
@@ -547,11 +547,11 @@
     near_x = own_g[...].astype(F32) + nn(back_own, xg[...])
     key_q = nt(q_rows, kvw[:, :D]).astype(BF)
     edge_x = nn(bedge_own, xg[...])
-    second_stage(0)
     arrived(C_XW)
     sn_x[...] = (edge_x + nn(bedge_side, rl_x[...])).astype(BF)
     send_lat(sn_x, rn_x, C_XS, north, south)
     near_x = near_x + nn(back_side, rl_x[...])
+    second_stage(0)
     second_stage(1)
     arrived(C_XS)
     arrived(C_AW)

time: 46.8 us -> 47.1 us (level)
  no operation moved by 1% of the time
where the time goes in v5:
time: 47.1 us; the launch traced here: 46.5 us
  Pallas kernels  44.9 us (95%)
  between operations  1.45 us (3%)
    pallas_call x1, Pallas kernels, local(): lax.cond(lon_shift[0] > WLON // 2, run(True), run(False), lev, latent_que...  43.8 us
    pallas_call x1, Pallas kernels, local(): pl.pallas_call(deliver, out_shape=shapes, in_specs=[hbm] * 4, out_specs=(...  1.1 us

profile of v5, /device:TPU:16, one launch (start us, length us, event | category | flops | bytes accessed | tf_op | source)
XLA Modules:
  0.0 46.5 jit_solution(12265117339115165119)
XLA Ops:
  1.3 44.0 %conditional.1 = ((bf16[72,2,512]{2,1,0:T(2,128)(2,1)S(1)}, bf16[72,13,512]{2,1,0:T(8,128)(2,1)S(1)}, f32[24,128]{1,0:T(8,128)S(1)}, f32[8,128]{1,0:T(8,128)S(1)})) conditional(s32[]{:T(128)} %bitcast, (bf16[72,13,512]{2,1,0:T(8,128)(2,1)}, bf16[2,512]{1,0:T(2,128)(2,1)}, bf16[512,1024]{1,0:T(8,128)(2,1)}, bf16[512,512]{1,0:T(8,128)(2,1)}, ...), branch_computations={%region_0.0_spmd, %region_1.0_spmd} | conditional | bytes 8 | solution.py:712
  1.3 43.8 %branch_0_fun.1 = (bf16[72,2,512]{2,1,0:T(2,128)(2,1)S(1)}, bf16[72,13,512]{2,1,0:T(8,128)(2,1)S(1)}, f32[24,128]{1,0:T(8,128)S(1)}, f32[8,128]{1,0:T(8,128)S(1)}) custom-call(bf16[72,13,512]{2,1,0:T(8,128)(2,1)} %get-tuple-element.48.lev_hbm, bf16[2,512]{1,0:T(2,128)(2,1)} %get-tuple-element.49.q_hbm, bf16[512,1024]{1,0:T(8,128)(2,1)} %get-tuple-element.50.kvw_hbm, ...), custom_call_target="tpu_custom_call" | custom-call | tf_op jit(solution)/shard_map/cond/branch_0_fun/pallas_call | solution.py:712
  45.3 1.1 %shard_map.147 = (bf16[72,2,512]{2,1,0:T(2,128)(2,1)}, bf16[72,13,512]{2,1,0:T(8,128)(2,1)}, f32[24,128]{1,0:T(8,128)}, f32[8,128]{1,0:T(8,128)}) custom-call(bf16[72,2,512]{2,1,0:T(2,128)(2,1)S(1)} %get-tuple-element.84.a, bf16[72,13,512]{2,1,0:T(8,128)(2,1)S(1)} %get-tuple-element.85.b, f32[24,128]{1,0:T(8,128)S(1)} %get-tuple-element.86.c, ...), custom_call_target="tpu_custom_call" | custom-call | tf_op jit(solution)/shard_map/pallas_call | solution.py:716
